TPU v7x, 128 devices: a whole 4x4x4 slice. The times are simulated.
128 devices in a mesh: ctx: 8 (over y_hi, z), tp: 16 (over x, y_lo, core).
Axes of the slice: x: 4, y: 4 (y_hi: 2, y_lo: 2; y = y_hi * 2 + y_lo), z: 4, core: 2. Of those that a mesh axis runs over, the one named last changes fastest.
Arguments:
- residual: bfloat16 [2048, 5376], P('ctx'), may hold values from -80 to 80
- stored_blocks: bfloat16 [896, 96, 768], P(('ctx', 'tp')), may hold values from -0.078125 to 0.078125
- block_list: int32 [896], replicated, may hold values from 0 to 895, as said below
- lengths: int32 [4], replicated, may hold values from 1 to 1536, 2048 in all
- in_gain: float32 [5376], replicated, may hold values from 0.5 to 1.5
- q_gain: float32 [128], replicated, may hold values from 0.25 to 1.75
- k_gain: float32 [128], replicated, may hold values from 0.25 to 1.75
- post_gain: float32 [5376], replicated, may hold values from 0.5 to 1.5
- final_gain: float32 [5376], replicated, may hold values from 0.5 to 1.5
- vocab_table: bfloat16 [147456, 5376], P(('ctx', 'tp')), may hold values from -1 to 1
- actions: int32 [2048], replicated, may hold values from 0 to 147455
- old_logprob: float32 [2048], P(('ctx', 'tp')), may hold values from -16 to -6
Outputs:
- ref_logprob: float32 [2048], P(('ctx', 'tp'))
- log_ratio: float32 [2048], P(('ctx', 'tp'))
Inputs may be any that keep to these rules, and one draw needn't show every extreme that they name: block_list holds every number of 0 to 895 once; the 7 slots of one storage device (slots d * 7 onward, d = its index over ctx+tp) belong to 7 different readers t, and the storage devices of one index of ctx together hold exactly 7 blocks of every reader.
All inputs are finite; a program needn't handle non-finite values.
Results may differ from a plain program's by a relative error of at most 0.0034.
Values may be sent and summed in bfloat16 or wider, within the bound.
A program may use at most 128 MiB of HBM per device.

v0:
```python
import jax
import jax.numpy as jnp
from jax import lax
from jax.sharding import PartitionSpec as P

HEADS = 32
KV_HEADS = 16
HEAD_DIM = 128
WINDOW = 1024
QUERY_SCALAR = 168


epsilon = 1e-06
soft_cap = 30.0
rope_base = 10000.0


def from_behind(value, axis, steps):
    count = lax.axis_size(axis)
    leading, last = (max(0, -steps), min(count, count - steps))
    return lax.ppermute(value, axis, [(source, source + steps) for source in range(leading, last)])


def rms_scale(values, gain_vec):
    mean_sq = jnp.mean(values * values, axis=-1, keepdims=True)
    return values * lax.rsqrt(mean_sq + epsilon) * gain_vec


def rotate(values, position):
    half_size = values.shape[-1] // 2
    frequency = rope_base ** (-2.0 * jnp.arange(half_size, dtype=jnp.float32) / values.shape[-1])
    angle_rows = position.astype(jnp.float32)[:, None] * frequency[None, :]
    cosine = jnp.cos(angle_rows)
    sine_part = jnp.sin(angle_rows)
    first_half = values[..., :half_size]
    second_half = values[..., half_size:]
    return jnp.concatenate(
        [
            first_half * cosine - second_half * sine_part,
            second_half * cosine + first_half * sine_part,
        ],
        axis=-1,
    )


def shards(
    residual,
    stored_blocks,
    block_list,
    lengths,
    in_gain,
    q_gain,
    k_gain,
    post_gain,
    final_gain,
    vocab_table,
    actions,
    old_logprob,
):
    ctx_count = lax.axis_size("ctx")
    tp_count = lax.axis_size("tp")
    ctx_index = lax.axis_index("ctx")
    tp_index = lax.axis_index("tp")
    device_index = lax.axis_index(("ctx", "tp"))
    row_count = residual.shape[0]
    blocks_dev = stored_blocks.shape[0]
    rows_per_reader = blocks_dev * ctx_count
    list_grid = block_list.reshape(ctx_count, tp_count, blocks_dev)
    reader_ids = list_grid // rows_per_reader
    row_index_all = list_grid % rows_per_reader
    my_list = lax.dynamic_index_in_dim(
        lax.dynamic_index_in_dim(list_grid, ctx_index, 0, False), tp_index, 0, False
    )
    my_readers = my_list // rows_per_reader
    send_mask = (my_readers[None, :] == jnp.arange(tp_count, dtype=jnp.int32)[:, None]).astype(
        jnp.bfloat16
    )
    outgoing = jnp.einsum(
        "tk,krc->trc", send_mask, stored_blocks, preferred_element_type=jnp.float32
    ).astype(jnp.bfloat16)
    incoming = lax.all_to_all(outgoing, "tp", split_axis=0, concat_axis=0, tiled=True)
    reader_hit = reader_ids == tp_index
    present = jnp.any(reader_hit, axis=2).astype(jnp.int32)
    row_index = jnp.sum(jnp.where(reader_hit, row_index_all, 0), axis=2)
    rank_ids = jnp.cumsum(present, axis=1) - 1
    choose_mask = (
        rank_ids[:, None, :] == jnp.arange(blocks_dev, dtype=jnp.int32)[None, :, None]
    ) & (present[:, None, :] == 1)
    kept_index = jnp.sum(jnp.where(choose_mask, row_index[:, None, :], 0), axis=2).reshape(-1)
    my_choose = lax.dynamic_index_in_dim(choose_mask, ctx_index, 0, False).astype(jnp.bfloat16)
    kept_blocks = jnp.einsum(
        "ks,src->krc", my_choose, incoming, preferred_element_type=jnp.float32
    ).astype(jnp.bfloat16)
    gathered = lax.all_gather(kept_blocks, "ctx", axis=0, tiled=True)
    slot_ids = jnp.arange(kept_index.shape[0], dtype=jnp.int32)
    placement = jnp.sum(
        jnp.where(
            kept_index[None, :] == jnp.arange(rows_per_reader, dtype=jnp.int32)[:, None],
            slot_ids[None, :],
            0,
        ),
        axis=1,
    )
    reader_weight = jnp.take(gathered, placement, axis=0).reshape(residual.shape[1], -1)
    query_width = HEADS // tp_count * HEAD_DIM
    key_width = KV_HEADS // tp_count * HEAD_DIM
    group_size = HEADS // KV_HEADS
    seq_starts = jnp.cumsum(lengths) - lengths
    query_ids = ctx_index * row_count + jnp.arange(row_count, dtype=jnp.int32)
    seg_start = jnp.max(
        jnp.where(seq_starts[None, :] <= query_ids[:, None], seq_starts[None, :], 0), axis=1
    )
    position = query_ids - seg_start
    normed = rms_scale(residual.astype(jnp.float32), in_gain).astype(jnp.bfloat16)
    projected = jnp.dot(
        normed, reader_weight[:, : query_width + 2 * key_width], preferred_element_type=jnp.float32
    )
    query_rows = projected[:, :query_width].reshape(row_count, -1, HEAD_DIM).transpose(1, 0, 2)
    key_rows = (
        projected[:, query_width : query_width + key_width]
        .reshape(row_count, -1, HEAD_DIM)
        .transpose(1, 0, 2)
    )
    value_rows = (
        projected[:, query_width + key_width :].reshape(row_count, -1, HEAD_DIM).transpose(1, 0, 2)
    )
    query_rows = rotate(rms_scale(query_rows, q_gain), position).astype(jnp.bfloat16)
    key_rows = rotate(rms_scale(key_rows, k_gain), position).astype(jnp.bfloat16)
    key_value = jnp.stack([key_rows, value_rows.astype(jnp.bfloat16)])
    reach_count = WINDOW // row_count
    earlier = [from_behind(key_value, "ctx", step_back) for step_back in range(reach_count, 0, -1)]
    before_rows = jnp.concatenate(earlier, axis=2)
    window_kv = jnp.concatenate([before_rows, key_value], axis=2)
    key_ids = (ctx_index - reach_count) * row_count + jnp.arange(
        window_kv.shape[2], dtype=jnp.int32
    )
    visible = (
        (key_ids[None, :] <= query_ids[:, None])
        & (query_ids[:, None] - key_ids[None, :] < WINDOW)
        & (key_ids[None, :] >= seg_start[:, None])
    )
    grouped = query_rows.reshape(-1, group_size, row_count, HEAD_DIM)
    scores = jnp.einsum(
        "hgqd,hkd->hgqk", grouped, window_kv[0], preferred_element_type=jnp.float32
    ) * QUERY_SCALAR ** (-0.5)
    prob_rows = jnp.where(visible, jnp.exp(scores), 0.0)
    prob_rows = (prob_rows / jnp.sum(prob_rows, axis=3, keepdims=True)).astype(jnp.bfloat16)
    mixed_out = jnp.einsum(
        "hgqk,hkd->hgqd", prob_rows, window_kv[1], preferred_element_type=jnp.float32
    ).astype(jnp.bfloat16)
    mixed_flat = (
        mixed_out.reshape(-1, row_count, HEAD_DIM)
        .transpose(1, 0, 2)
        .reshape(row_count, query_width)
    )
    out_columns = reader_weight[:, query_width + 2 * key_width :]
    vocab_rows = vocab_table.shape[0]
    vocab_ids = device_index * vocab_rows + jnp.arange(vocab_rows, dtype=jnp.int32)
    share_rows = row_count // tp_count
    summed = lax.psum_scatter(
        lax.dot_general(
            mixed_flat, out_columns, (((1,), (1,)), ((), ())), preferred_element_type=jnp.float32
        ),
        "tp",
        scatter_dimension=0,
        tiled=True,
    )
    own_rows = lax.dynamic_slice_in_dim(residual, tp_index * share_rows, share_rows, 0)
    hidden = own_rows.astype(jnp.float32) + rms_scale(summed, post_gain)
    logits = lax.dot_general(
        lax.all_gather(
            rms_scale(hidden, final_gain).astype(jnp.bfloat16), ("ctx", "tp"), axis=0, tiled=True
        ),
        vocab_table,
        (((1,), (1,)), ((), ())),
        preferred_element_type=jnp.float32,
    )
    capped = soft_cap * jnp.tanh(logits / soft_cap)
    hit_mask = vocab_ids[None, :] == actions[:, None]
    vocab_stats = jnp.stack(
        [jnp.sum(jnp.exp(capped), axis=1), jnp.sum(jnp.where(hit_mask, capped, 0.0), axis=1)]
    )
    totals = lax.psum(vocab_stats, ("ctx", "tp"))
    my_stats = lax.dynamic_slice_in_dim(totals, device_index * share_rows, share_rows, 1)
    ref_logprob = my_stats[1] - jnp.log(my_stats[0])
    return (ref_logprob, old_logprob - ref_logprob)


def solution(mesh):
    return jax.shard_map(
        shards,
        mesh=mesh,
        in_specs=(
            P("ctx", None),
            P(("ctx", "tp"), None, None),
            P(),
            P(),
            P(),
            P(),
            P(),
            P(),
            P(),
            P(("ctx", "tp"), None),
            P(),
            P(("ctx", "tp")),
        ),
        out_specs=(P(("ctx", "tp")), P(("ctx", "tp"))),
        check_vma=False,
    )
```

profile of v0, /device:TPU:1, one launch (start us, length us, event | category | flops | bytes accessed | tf_op | source)
XLA Modules:
  0.0 609.0 jit_solution(15948201727695070497)
XLA Ops:
  7.2 1.0 reshape.369
  8.4 1.3 convolution_convert_fusion
  9.7 2.2 copy.26
  11.9 7.0 %all-to-all-start = ((bf16[16,96,768]{2,1,0:T(8,128)(2,1)}), bf16[16,96,768]{2,1,0:T(8,128)(2,1)S(1)}, u32[]{:S(2)}, u32[]{:S(2)}) async-start(bf16[16,96,768]{2,1,0:T(8,128)(2,1)} %copy.26), calls=%async_computation | async-start | bytes 4718592 | tf_op jit(solution)/shard_map/all_to_all | solution.py:81
  19.6 29.5 %all-to-all-done = bf16[16,96,768]{2,1,0:T(8,128)(2,1)S(1)} async-done(((bf16[16,96,768]{2,1,0:T(8,128)(2,1)}), bf16[16,96,768]{2,1,0:T(8,128)(2,1)S(1)}, u32[]{:S(2)}, u32[]{:S(2)}) %all-to-all-start) | async-done | bytes 2359328 | tf_op jit(solution)/shard_map/all_to_all | solution.py:81
  49.1 1.4 fusion.14
  50.5 1.2 copy.28
  52.8 2.4 fusion
  55.2 0.5 multiply_cosine_fusion.1
  55.7 0.4 fusion.20
  56.2 103.5 %all-gather.3.cloned.1.call-done = bf16[56,96,768]{2,1,0:T(8,128)(2,1)} async-done(((bf16[7,96,768]{2,1,0:T(8,128)(2,1)}), bf16[56,96,768]{2,1,0:T(8,128)(2,1)}) %all-gather.3.cloned.1.call-update) | async-done | bytes 8257552 | tf_op jit(solution)/shard_map/all_gather | solution.py:94
  159.7 9.0 %gather_fusion = bf16[56,96,768]{2,1,0:T(8,128)(2,1)} fusion(bf16[56,96,768]{2,1,0:T(8,128)(2,1)} %all-gather.3.cloned.1.call-done, s32[1024]{0:T(1024)S(1)} %pad_clamp_fusion), kind=kCustom, calls=%fused_computation | custom fusion | bytes 16515296 | tf_op jit(solution)/shard_map/jit(_take)/gather | solution.py:104
  168.7 5.6 bitcast_select_fusion
  174.3 1.6 fusion.3
  176.0 1.5 copy-done.2
  177.9 0.6 fusion.43
  178.6 2.1 collective-permute-start
  180.7 2.4 collective-permute-start.1
  183.1 2.2 collective-permute-start.2
  185.3 2.5 collective-permute-start.3
  188.2 2.2 collective-permute-done.3
  190.6 2.4 fusion.6
  192.9 3.3 fusion.22
  196.3 5.2 fusion.8
  201.6 73.9 %reduce-scatter.2.cloned.1.call-done = f32[16,5376]{1,0:T(8,128)} async-done(((f32[256,5376]{1,0:T(8,128)}), f32[16,5376]{1,0:T(8,128)}) %reduce-scatter.2.cloned.1.call-update) | async-done | bytes 344080 | tf_op jit(solution)/shard_map/reduce_scatter | solution.py:160
  275.5 1.1 multiply_reduce_fusion.1
  276.6 1.3 multiply_reduce_fusion
  277.9 1.8 multiply_convert_fusion
  279.8 223.5 %all-gather.5.cloned.1.call-done = bf16[2048,5376]{1,0:T(8,128)(2,1)} async-done(((bf16[16,5376]{1,0:T(8,128)(2,1)}), bf16[2048,5376]{1,0:T(8,128)(2,1)}) %all-gather.5.cloned.1.call-update) | async-done | bytes 22020112 | tf_op jit(solution)/shard_map/all_gather | solution.py:171
  503.3 34.9 %exponential_reduce_fusion = (f32[2048]{0:T(1024)S(1)}, f32[2048]{0:T(1024)S(1)}) fusion(s32[2048]{0:T(1024)S(1)} %copy-done.10, s32[1152]{0:T(1024)S(1)} %iota_add_fusion, bf16[2048,5376]{1,0:T(8,128)(2,1)} %all-gather.5.cloned.1.call-done, bf16[1152,5376]{1,0:T(8,128)(2,1)} %param.21), kind=kOutput, calls=%fused_computation.3 | convolution fusion | flops 25381302272 | bytes 34435584 | tf_op jit(solution)/shard_map/dot_general | solution.py:170
  538.2 63.6 %psum.7 = f32[2,2048]{1,0:T(2,128)S(1)} all-reduce(f32[2,2048]{1,0:T(2,128)S(1)} %pad_maximum_fusion.1), channel_id=1, replica_groups=mesh['ctx'=8,'tp'=16] {'ctx','tp'}, use_global_device_ids=true, to_apply=%region_16.17 | all-reduce | flops 4096 | bytes 32768 | tf_op jit(solution)/shard_map/psum | solution.py:183
  601.9 0.5 fusion.55
  (74 shorter events, 3.1 us)
Async XLA Ops:
  7.2 1.2 copy-start
  11.9 40.5 %copy-start.11 = (s32[4]{0:T(128)S(1)}, s32[4]{0:T(128)}, u32[]{:S(2)}) copy-start(s32[4]{0:T(128)} %param.15) | copy-start | bytes 52
  11.9 37.2 %all-to-all-start = ((bf16[16,96,768]{2,1,0:T(8,128)(2,1)}), bf16[16,96,768]{2,1,0:T(8,128)(2,1)S(1)}, u32[]{:S(2)}, u32[]{:S(2)}) async-start(bf16[16,96,768]{2,1,0:T(8,128)(2,1)} %copy.26), calls=%async_computation | async-start | bytes 4718592 | tf_op jit(solution)/shard_map/all_to_all | solution.py:81
  18.9 140.8 %all-gather.3.cloned.1.call-start = ((), (), s32[]{:S(2)}) async-start(), calls=%async_computation.2 | async-start | bytes 9289728 | tf_op jit(solution)/shard_map/all_gather | solution.py:94
  51.8 223.7 %reduce-scatter.2.cloned.1.call-start = ((), (), s32[]{:S(2)}) async-start(), calls=%async_computation.3 | async-start | bytes 5849088 | tf_op jit(solution)/shard_map/reduce_scatter | solution.py:160
  168.7 5.6 copy-start.3
  168.7 5.6 copy-start.9
  174.3 3.2 copy-start.2
  174.3 3.5 copy-start.6
  174.3 13.5 %copy-start.7 = (f32[128]{0:T(128)S(1)}, f32[128]{0:T(128)}, u32[]{:S(2)}) copy-start(f32[128]{0:T(128)} %param.17) | copy-start | bytes 1540
  178.6 9.6 %collective-permute-start = (bf16[2,1,256,128]{3,2,1,0:T(8,128)(2,1)S(1)}, bf16[2,1,256,128]{3,2,1,0:T(8,128)(2,1)S(1)}, u32[]{:S(2)}, u32[]{:S(2)}) collective-permute-start(bf16[2,1,256,128]{3,2,1,0:T(8,128)(2,1)S(1)} %pad_maximum_fusion), channel_id=1, source_target_pairs={{0,64},{16,80},{32,96},{48,112},{1,65},{17,81},{33,97},{49,113},{2... | collective-permute-start | bytes 393224 | tf_op jit(solution)/shard_map/ppermute | solution.py:21
  180.7 7.4 %collective-permute-start.1 = (bf16[2,1,256,128]{3,2,1,0:T(8,128)(2,1)S(1)}, bf16[2,1,256,128]{3,2,1,0:T(8,128)(2,1)S(1)}, u32[]{:S(2)}, u32[]{:S(2)}) collective-permute-start(bf16[2,1,256,128]{3,2,1,0:T(8,128)(2,1)S(1)} %pad_maximum_fusion), channel_id=1, source_target_pairs={{0,48},{16,64},{32,80},{48,96},{64,112},{1,49},{17,65},{33,81},{49... | collective-permute-start | bytes 393224 | tf_op jit(solution)/shard_map/ppermute | solution.py:21
  183.1 5.1 collective-permute-start.2
  185.3 5.1 collective-permute-start.3
  201.5 75.1 %copy-start.4 = (f32[5376]{0:T(1024)S(1)}, f32[5376]{0:T(1024)}, u32[]{:S(2)}) copy-start(f32[5376]{0:T(1024)} %param.19) | copy-start | bytes 64516
  201.5 76.4 %copy-start.5 = (f32[5376]{0:T(1024)S(1)}, f32[5376]{0:T(1024)}, u32[]{:S(2)}) copy-start(f32[5376]{0:T(1024)} %param.20) | copy-start | bytes 64516
  201.5 301.8 %copy-start.10 = (s32[2048]{0:T(1024)S(1)}, s32[2048]{0:T(1024)}, u32[]{:S(2)}) copy-start(s32[2048]{0:T(1024)} %param.22) | copy-start | bytes 24580
  201.5 301.8 %all-gather.5.cloned.1.call-start = ((), (), s32[]{:S(2)}) async-start(), calls=%async_computation.4 | async-start | bytes 22192128 | tf_op jit(solution)/shard_map/all_gather | solution.py:171
  279.8 322.1 %copy-start.8 = (f32[16]{0:T(128)S(1)}, f32[16]{0:T(128)}, u32[]{:S(2)}) copy-start(f32[16]{0:T(128)} %param.23) | copy-start | bytes 196
  503.3 99.2 %copy-start.1 = (bf16[7,96,768]{2,1,0:T(8,128)(2,1)S(1)}, bf16[7,96,768]{2,1,0:T(8,128)(2,1)}, u32[]{:S(2)}) copy-start(bf16[7,96,768]{2,1,0:T(8,128)(2,1)} %param.13) | copy-start | bytes 3096580
Sparse Core Ops, SparseCore 0:
  51.9 107.7 all-gather.2
  201.6 73.7 reduce-scatter.1
  279.9 223.3 all-gather.4
where the time goes:
time: 610 us; the launch traced here: 609 us
  waiting for transfers between devices  433 us (71%)
  blocking collectives  63.6 us (10%)
  matrix products  50.1 us (8%)
  other arithmetic  16.5 us (3%)
  starting transfers between devices  16.3 us (3%)
  local copies, waits for them, and re-layouts  15.6 us (3%)
  between operations  14.2 us (2%)
    all_gather x1, waiting for transfers between devices, shards(): lax.all_gather(rms_scale(hidden, final_gain).astype(jnp.bfloat16), ('ctx'...  223 us
    all_gather x1, waiting for transfers between devices, shards(): gathered = lax.all_gather(kept_blocks, 'ctx', axis=0, tiled=True)  104 us
    reduce_scatter x1, waiting for transfers between devices, shards(): lax.psum_scatter(lax.dot_general(mixed_flat, out_columns, (((1,), (1,)),...  73.9 us
    psum x1, blocking collectives, shards(): totals = lax.psum(vocab_stats, ('ctx', 'tp'))  63.6 us
    dot_general x1, matrix products, shards(): lax.dot_general(lax.all_gather(rms_scale(hidden, final_gain).astype(jnp.b...  34.9 us
    all_to_all x1, waiting for transfers between devices, shards(): lax.all_to_all(outgoing, 'tp', split_axis=0, concat_axis=0, tiled=True)  29.5 us
  transfers between devices with their start and end apart: 8, of which 5 were waited for; matrix products, arithmetic and copies ran while one was open for 1% of the time, Pallas kernels for 0%

commit v1 on v0

--- a/solution.py
+++ b/solution.py
@@ -1,6 +1,8 @@
 import jax
 import jax.numpy as jnp
 from jax import lax
+from jax.experimental import pallas as pl
+from jax.experimental.pallas import tpu as pltpu
 from jax.sharding import PartitionSpec as P
 
 HEADS = 32
@@ -13,6 +15,316 @@
 epsilon = 1e-06
 soft_cap = 30.0
 rope_base = 10000.0
+MESH = pl.DeviceIdType.MESH
+VMEM = pltpu.VMEM
+A2_REL = (0, 1, 3, 2)
+
+
+def coords():
+    c = lax.axis_index("ctx")
+    t = lax.axis_index("tp")
+    return t // 4, (c // 4) * 2 + (t // 2) % 2, c % 4, t % 2
+
+
+def device_of(x, y, z, k):
+    x, y, z, k = x % 4, y % 4, z % 4, k % 2
+    return ((y // 2) * 4 + z, x * 4 + (y % 2) * 2 + k)
+
+
+def axis_of(part, place):
+    return (part + place) % 3
+
+
+def shifted(axis, steps):
+    where = list(coords())
+    where[axis] = where[axis] + steps
+    return device_of(*where)
+
+
+def sibling():
+    x, y, z, k = coords()
+    return device_of(x, y, z, k + 1)
+
+
+def greet(peers):
+    barrier = pltpu.get_barrier_semaphore()
+    for peer in peers:
+        pl.semaphore_signal(barrier, inc=1, device_id=peer, device_id_type=MESH)
+    pl.semaphore_wait(barrier, len(peers))
+
+
+def vocab_kernel(
+    fin_ref, table_ref, actions_ref, out_ref,
+    buf, table, acc, part_exp, part_hit, st1, r1, st2, r2,
+    table_sem, s1, v1, s2, v2, s3, v3, sf, vf, sk, vk, sa, va, sb, vb,
+):
+    ctx = lax.axis_index("ctx")
+    tp = lax.axis_index("tp")
+    core = tp % 2
+    own = coords()[:3]
+    width = fin_ref.shape[1] // 3
+    rows = fin_ref.shape[0]
+    vocab_rows = table.shape[1]
+
+    def table_copy(p):
+        return pltpu.make_async_copy(
+            table_ref.at[:, pl.ds(p * width, width)], table.at[p], table_sem.at[p]
+        )
+
+    for p in range(3):
+        table_copy(p).start()
+    for p in range(3):
+        buf[p, 0, 0, core, 0] = fin_ref[:, pl.ds(p * width, width)]
+    x, y, z, k = coords()
+    c_peer = lambda off: ((ctx + off) % 8, tp)
+    t_peer = lambda off: (ctx, (tp + off) % 16)
+    far_y = device_of(x, y - 1 + 2 * (y % 2), z, k)
+    greet([c_peer(o) for o in range(1, 8)] + [t_peer(o) for o in range(1, 16)] + [far_y])
+
+    def send(src, dst, send_sem, recv_sem, peer):
+        return pltpu.make_async_remote_copy(
+            src_ref=src, dst_ref=dst, send_sem=send_sem, recv_sem=recv_sem,
+            device_id=peer, device_id_type=MESH,
+        )
+
+    def first(p, step):
+        return send(
+            buf.at[p, 0, 0, core, 0], buf.at[p, 0, 0, core, 4 - step],
+            s1.at[p, step - 1], v1.at[p, step - 1], shifted(axis_of(p, 0), step),
+        )
+
+    def second(p, step):
+        slot = A2_REL.index(4 - step)
+        return send(
+            buf.at[p, 0, 0, core], buf.at[p, 0, slot, core],
+            s2.at[p, slot], v2.at[p, slot], shifted(axis_of(p, 1), step),
+        )
+
+    def third(p, q, step):
+        return send(
+            buf.at[p, 0, q, core], buf.at[p, 4 - step, q, core],
+            s3.at[p, 4 - step, q], v3.at[p, 4 - step, q], shifted(axis_of(p, 2), step),
+        )
+
+    def passed(p, slab, q, step):
+        return send(
+            buf.at[p, slab, q, core], buf.at[p, 2, q, core],
+            sf.at[p, q], vf.at[p, q], shifted(axis_of(p, 2), step),
+        )
+
+    def across(p, slab, q):
+        return send(
+            buf.at[p, slab, q, core], buf.at[p, slab, q, core],
+            sk.at[p, slab, q], vk.at[p, slab, q], sibling(),
+        )
+
+    for p in range(3):
+        for step in (1, 3, 2):
+            first(p, step).start()
+    for p in range(3):
+        for step in (1, 3, 2):
+            first(p, step).wait_recv()
+        for step in (3, 1, 2):
+            second(p, step).start()
+    for p in range(3):
+        for step in (1, 3):
+            third(p, 0, step).start()
+        across(p, 0, 0).start()
+
+    def own_chunk(p, q):
+        second(p, 4 - A2_REL[q]).wait_recv()
+        for step in (1, 3):
+            third(p, q, step).start()
+        across(p, 0, q).start()
+
+    for p in range(3):
+        own_chunk(p, 1)
+
+    def slab_of(g):
+        return jnp.where(g < 2, 0, jnp.where(g > 5, 2, jnp.where(g % 2 == 0, 3, 1)))
+
+    def half_of(g):
+        return jnp.where(g < 2, g, jnp.where(g > 5, g - 6, (g - 2) // 2))
+
+    def arrivals(g):
+        slab, half = slab_of(g), half_of(g)
+
+        @pl.when(g == 1)
+        def _():
+            for q in (2, 3):
+                for p in range(3):
+                    own_chunk(p, q)
+
+        @pl.when((g > 1) & (g < 6))
+        def _():
+            for i in range(2):
+                q = half * 2 + i
+                for p in range(3):
+                    pltpu.make_async_remote_copy(
+                        src_ref=buf.at[p, 0, q, core], dst_ref=buf.at[p, slab, q, core],
+                        send_sem=s3.at[p, slab, q], recv_sem=v3.at[p, slab, q],
+                        device_id=sibling(), device_id_type=MESH,
+                    ).wait_recv()
+                    if i == 0:
+                        @pl.when(slab == 3)
+                        def _():
+                            passed(p, 3, q, 1).start()
+                    else:
+                        @pl.when(slab == 1)
+                        def _():
+                            passed(p, 1, q, 3).start()
+                    across(p, slab, q).start()
+
+        @pl.when((g > 5) & (g < 8))
+        def _():
+            for i in range(2):
+                q = half * 2 + i
+                for p in range(3):
+                    passed(p, 3, q, 1).wait_recv()
+                    across(p, 2, q).start()
+
+    def place(axis_values, k):
+        x, y, z = axis_values
+        return ((y // 2) * 4 + z) * 16 + x * 4 + (y % 2) * 2 + k
+
+    def group(g, carry):
+        slab, half = slab_of(g), half_of(g)
+        for p in range(3):
+            for i in range(2):
+                across(p, slab, half * 2 + i).wait_recv()
+
+            @pl.when(g == 0)
+            def _():
+                table_copy(p).wait()
+
+            lhs = buf[p, slab, pl.ds(half * 2, 2)].reshape(16 * rows, width)
+            got = lax.dot_general(
+                lhs, table[p], (((1,), (1,)), ((), ())), preferred_element_type=jnp.float32
+            )
+            a1, a2, a3 = (axis_of(p, i) for i in range(3))
+            for i in range(2):
+                q = half * 2 + i
+                rel2 = jnp.where(q < 2, q, 5 - q)
+                for kk in range(2):
+                    for r1_ in range(4):
+                        at = [None] * 3
+                        at[a1] = (own[a1] + r1_) % 4
+                        at[a2] = (own[a2] + rel2) % 4
+                        at[a3] = (own[a3] + slab) % 4
+                        d = place(at, kk)
+                        m = (i * 2 + kk) * 4 + r1_
+                        value = got[m * rows:(m + 1) * rows]
+                        acc[d] = acc[d] + value
+            if p == 0:
+                arrivals(g + 1)
+        return carry
+
+    def clear(d, carry):
+        acc[d] = jnp.zeros((rows, vocab_rows), jnp.float32)
+        return carry
+
+    lax.fori_loop(0, 128, clear, 0)
+    lax.fori_loop(0, 8, group, 0)
+
+    first_id = (ctx * 16 + tp) * vocab_rows
+    ids = first_id + lax.broadcasted_iota(jnp.int32, (rows, vocab_rows), 1)
+
+    def fold(v):
+        total = v[:, :128]
+        for i in range(1, vocab_rows // 128):
+            total = total + v[:, i * 128:(i + 1) * 128]
+        return total
+
+    def tail(d, carry):
+        capped = soft_cap * jnp.tanh(acc[d] * (1.0 / soft_cap))
+        hit = ids == actions_ref[d]
+        part_exp[d] = fold(jnp.exp(capped))
+        part_hit[d] = fold(jnp.where(hit, capped, 0.0))
+        return carry
+
+    lax.fori_loop(0, 128, tail, 0)
+    ones = jnp.ones((8, 128), jnp.float32)
+    for c in range(8):
+        for row, part in ((0, part_exp), (1, part_hit)):
+            got = lax.dot_general(
+                ones, part[pl.ds(c * 16, 16)].reshape(16 * rows, 128), (((1,), (1,)), ((), ())),
+                preferred_element_type=jnp.float32, precision=lax.Precision.HIGHEST,
+            )
+            st1[c, row * 8:(row + 1) * 8, :] = got
+    def stage1(off):
+        return send(st1.at[(ctx + off) % 8], r1.at[off], sa.at[off], va.at[off], c_peer(off))
+
+    def stage2(off):
+        return send(st2, r2.at[off], sb.at[off], vb.at[off], t_peer(off))
+
+    for off in range(1, 8):
+        stage1(off).start()
+    total = st1[ctx]
+    for off in range(1, 8):
+        stage1(off).wait_recv()
+        total = total + r1[off]
+    st2[...] = total
+    for off in range(1, 16):
+        stage2(off).start()
+    for off in range(1, 16):
+        stage2(off).wait_recv()
+        total = total + r2[off]
+    out_ref[...] = total[8:] - jnp.log(total[:8])
+
+    for p in range(3):
+        for step in (1, 2, 3):
+            first(p, step).wait_send()
+            second(p, step).wait_send()
+        for q in range(4):
+            third(p, q, 1).wait_send()
+            third(p, q, 3).wait_send()
+            passed(p, 3, q, 1).wait_send()
+            for slab in range(4):
+                across(p, slab, q).wait_send()
+    for off in range(1, 8):
+        stage1(off).wait_send()
+    for off in range(1, 16):
+        stage2(off).wait_send()
+
+
+def vocab_stats(fin, table, actions):
+    rows, depth = fin.shape
+    width = depth // 3
+    vocab_rows = table.shape[0]
+    dma = pltpu.SemaphoreType.DMA
+    return pl.pallas_call(
+        vocab_kernel,
+        out_shape=jax.ShapeDtypeStruct((8, 16 * rows), jnp.float32),
+        in_specs=[
+            pl.BlockSpec(memory_space=VMEM),
+            pl.BlockSpec(memory_space=pl.ANY),
+            pl.BlockSpec(memory_space=VMEM),
+        ],
+        out_specs=pl.BlockSpec(memory_space=VMEM),
+        scratch_shapes=[
+            VMEM((3, 4, 4, 2, 4, rows, width), jnp.bfloat16),
+            VMEM((3, vocab_rows, width), jnp.bfloat16),
+            VMEM((128, rows, vocab_rows), jnp.float32),
+            VMEM((128, rows, 128), jnp.float32),
+            VMEM((128, rows, 128), jnp.float32),
+            VMEM((8, 16, 16 * rows), jnp.float32),
+            VMEM((8, 16, 16 * rows), jnp.float32),
+            VMEM((16, 16 * rows), jnp.float32),
+            VMEM((16, 16, 16 * rows), jnp.float32),
+            dma((3,)),
+            dma((3, 3)), dma((3, 3)),
+            dma((3, 4)), dma((3, 4)),
+            dma((3, 4, 4)), dma((3, 4, 4)),
+            dma((3, 4)), dma((3, 4)),
+            dma((3, 4, 4)), dma((3, 4, 4)),
+            dma((8,)), dma((8,)),
+            dma((16,)), dma((16,)),
+        ],
+        compiler_params=pltpu.CompilerParams(
+            collective_id=2, has_side_effects=True, vmem_limit_bytes=60 * 2**20
+        ),
+        name="vocab_stats",
+    )(fin, table, actions.reshape(128, rows, 1))
 
 
 def from_behind(value, axis, steps):
@@ -61,7 +373,6 @@
     tp_count = lax.axis_size("tp")
     ctx_index = lax.axis_index("ctx")
     tp_index = lax.axis_index("tp")
-    device_index = lax.axis_index(("ctx", "tp"))
     row_count = residual.shape[0]
     blocks_dev = stored_blocks.shape[0]
     rows_per_reader = blocks_dev * ctx_count
@@ -154,8 +465,6 @@
         .reshape(row_count, query_width)
     )
     out_columns = reader_weight[:, query_width + 2 * key_width :]
-    vocab_rows = vocab_table.shape[0]
-    vocab_ids = device_index * vocab_rows + jnp.arange(vocab_rows, dtype=jnp.int32)
     share_rows = row_count // tp_count
     summed = lax.psum_scatter(
         lax.dot_general(
@@ -167,22 +476,9 @@
     )
     own_rows = lax.dynamic_slice_in_dim(residual, tp_index * share_rows, share_rows, 0)
     hidden = own_rows.astype(jnp.float32) + rms_scale(summed, post_gain)
-    logits = lax.dot_general(
-        lax.all_gather(
-            rms_scale(hidden, final_gain).astype(jnp.bfloat16), ("ctx", "tp"), axis=0, tiled=True
-        ),
-        vocab_table,
-        (((1,), (1,)), ((), ())),
-        preferred_element_type=jnp.float32,
-    )
-    capped = soft_cap * jnp.tanh(logits / soft_cap)
-    hit_mask = vocab_ids[None, :] == actions[:, None]
-    vocab_stats = jnp.stack(
-        [jnp.sum(jnp.exp(capped), axis=1), jnp.sum(jnp.where(hit_mask, capped, 0.0), axis=1)]
-    )
-    totals = lax.psum(vocab_stats, ("ctx", "tp"))
-    my_stats = lax.dynamic_slice_in_dim(totals, device_index * share_rows, share_rows, 1)
-    ref_logprob = my_stats[1] - jnp.log(my_stats[0])
+    final = rms_scale(hidden, final_gain).astype(jnp.bfloat16)
+    all_rows = vocab_stats(final, vocab_table, actions)
+    ref_logprob = lax.dynamic_slice_in_dim(all_rows[0], tp_index * share_rows, share_rows, 0)
     return (ref_logprob, old_logprob - ref_logprob)
 
 

time: 610 us -> 379 us (0.62)
  waiting for transfers between devices: 433 us -> 207 us
  Pallas kernels: 0 us -> 90.6 us
  blocking collectives: 63.6 us -> 0 us
  matrix products: 50.1 us -> 15.2 us
    all_gather x1 -> x0, waiting for transfers between devices: 223 us -> none  [shards(): lax.all_gather(rms_scale(hidden, final_gain).astype(jnp.bfloat16), ('ctx'...]
    pallas_call x0 -> x1, Pallas kernels: none -> 90.6 us  [vocab_stats(): pl.pallas_call(vocab_kernel, out_shape=jax.ShapeDtypeStruct((8, 16 * rows...]
    psum x1 -> x0, blocking collectives: 63.6 us -> none  [shards(): totals = lax.psum(vocab_stats, ('ctx', 'tp'))]
    dot_general x1 -> x0, matrix products: 34.9 us -> none  [shards(): lax.dot_general(lax.all_gather(rms_scale(hidden, final_gain).astype(jnp.b...]
  transfers between devices with their start and end apart: 8 -> 7, of which waited for: 5 -> 4; matrix products, arithmetic and copies ran while one was open for 1% -> 2% of each run, Pallas kernels for 0% -> 0%
where the time goes in v1:
time: 379 us
  waiting for transfers between devices  207 us (55%)
  Pallas kernels  90.6 us (24%)
  local copies, waits for them, and re-layouts  18.7 us (5%)
  other arithmetic  16.6 us (4%)
  starting transfers between devices  16.1 us (4%)
  matrix products  15.2 us (4%)
  between operations  14.4 us (4%)
    all_gather x1, waiting for transfers between devices, shards(): gathered = lax.all_gather(kept_blocks, 'ctx', axis=0, tiled=True)  104 us
    pallas_call x1, Pallas kernels, vocab_stats(): pl.pallas_call(vocab_kernel, out_shape=jax.ShapeDtypeStruct((8, 16 * rows...  90.6 us
    reduce_scatter x1, waiting for transfers between devices, shards(): lax.psum_scatter(lax.dot_general(mixed_flat, out_columns, (((1,), (1,)),...  71.6 us
    all_to_all x1, waiting for transfers between devices, shards(): lax.all_to_all(outgoing, 'tp', split_axis=0, concat_axis=0, tiled=True)  29.5 us
    ppermute x4, starting transfers between devices, from_behind(): lax.ppermute(value, axis, [(source, source + steps) for source in range(l...  9.2 us
    gather x1, local copies, waits for them, and re-layouts, shards(): jnp.take(gathered, placement, axis=0).reshape(residual.shape[1], -1)  9 us
  transfers between devices with their start and end apart: 7, of which 4 were waited for; matrix products, arithmetic and copies ran while one was open for 2% of the time, Pallas kernels for 0%

profile of v1, /device:TPU:1, one launch (start us, length us, event | category | flops | bytes accessed | tf_op | source)
XLA Modules:
  0.0 378.6 jit_solution(2713276136506872113)
XLA Ops:
  7.2 1.0 reshape.366
  8.4 1.3 convolution_convert_fusion
  9.7 2.2 copy.28
  11.9 6.8 %all-to-all-start = ((bf16[16,96,768]{2,1,0:T(8,128)(2,1)}), bf16[16,96,768]{2,1,0:T(8,128)(2,1)S(1)}, u32[]{:S(2)}, u32[]{:S(2)}) async-start(bf16[16,96,768]{2,1,0:T(8,128)(2,1)} %copy.28), calls=%async_computation | async-start | bytes 4718592 | tf_op jit(solution)/shard_map/all_to_all | solution.py:392
  19.5 29.5 %all-to-all-done = bf16[16,96,768]{2,1,0:T(8,128)(2,1)S(1)} async-done(((bf16[16,96,768]{2,1,0:T(8,128)(2,1)}), bf16[16,96,768]{2,1,0:T(8,128)(2,1)S(1)}, u32[]{:S(2)}, u32[]{:S(2)}) %all-to-all-start) | async-done | bytes 2359328 | tf_op jit(solution)/shard_map/all_to_all | solution.py:392
  49.0 1.4 fusion.14
  50.4 1.2 copy.30
  52.6 2.4 fusion
  55.1 0.5 multiply_cosine_fusion.1
  56.1 103.5 %all-gather.2.cloned.1.call-done = bf16[56,96,768]{2,1,0:T(8,128)(2,1)} async-done(((bf16[7,96,768]{2,1,0:T(8,128)(2,1)}), bf16[56,96,768]{2,1,0:T(8,128)(2,1)}) %all-gather.2.cloned.1.call-update) | async-done | bytes 8257552 | tf_op jit(solution)/shard_map/all_gather | solution.py:405
  159.6 9.0 %gather_fusion = bf16[56,96,768]{2,1,0:T(8,128)(2,1)} fusion(bf16[56,96,768]{2,1,0:T(8,128)(2,1)} %all-gather.2.cloned.1.call-done, s32[1024]{0:T(1024)S(1)} %pad_clamp_fusion), kind=kCustom, calls=%fused_computation | custom fusion | bytes 16515296 | tf_op jit(solution)/shard_map/jit(_take)/gather | solution.py:415
  168.6 5.6 %bitcast_select_fusion = bf16[5376,768]{1,0:T(8,128)(2,1)S(1)} fusion(bf16[56,96,768]{2,1,0:T(8,128)(2,1)} %gather_fusion, pred[5376]{0:T(1024)(128)(4,1)S(1)} %broadcast_in_dim.63), kind=kLoop, calls=%fused_computation.1 | loop fusion | flops 4128768 | bytes 16520448 | tf_op jit(solution)/shard_map/jit(_take)/select_n | solution.py:415
  174.2 1.6 fusion.3
  175.8 1.5 copy-done.1
  177.8 0.6 fusion.43
  178.4 2.1 collective-permute-start
  180.6 2.4 collective-permute-start.1
  183.0 2.2 collective-permute-start.2
  185.2 2.5 collective-permute-start.3
  188.1 2.2 collective-permute-done.3
  190.4 2.4 fusion.6
  192.8 3.3 fusion.22
  196.2 5.2 %fusion.8 = f32[256,5376]{1,0:T(8,128)} fusion(bf16[256,256]{0,1:T(8,128)(2,1)S(1)} %bitcast.70, bf16[5376,768]{1,0:T(8,128)(2,1)} %copy-done.1), kind=kOutput, calls=%fused_computation.12 | convolution fusion | flops 704643072 | bytes 8388608 | tf_op jit(solution)/shard_map/dot_general | solution.py:470
  201.4 0.7 copy-done.5
  202.0 1.9 reshape.384.actions_ref
  203.9 71.6 %reduce-scatter.2.cloned.1.call-done = f32[16,5376]{1,0:T(8,128)} async-done(((f32[256,5376]{1,0:T(8,128)}), f32[16,5376]{1,0:T(8,128)}) %reduce-scatter.2.cloned.1.call-update) | async-done | bytes 344080 | tf_op jit(solution)/shard_map/reduce_scatter | solution.py:469
  275.5 1.1 multiply_reduce_fusion.1
  276.7 1.3 multiply_reduce_fusion
  278.0 1.9 multiply_convert_fusion.fin_ref
  279.8 90.6 %vocab_stats.1 = f32[8,256]{1,0:T(8,128)} custom-call(bf16[16,5376]{1,0:T(8,128)(2,1)} %multiply_convert_fusion.fin_ref, bf16[1152,5376]{1,0:T(8,128)(2,1)} %table_ref.1, s32[128,16,1]{2,1,0:T(8,128)} %reshape.384.actions_ref), custom_call_target="tpu_custom_call" | custom-call | tf_op jit(solution)/shard_map/vocab_stats/pallas_call | solution.py:295
  370.5 0.7 slice.48
  371.2 0.6 fusion.56
  (67 shorter events, 3.4 us)
Async XLA Ops:
  7.2 1.2 copy-start
  11.9 37.1 %all-to-all-start = ((bf16[16,96,768]{2,1,0:T(8,128)(2,1)}), bf16[16,96,768]{2,1,0:T(8,128)(2,1)S(1)}, u32[]{:S(2)}, u32[]{:S(2)}) async-start(bf16[16,96,768]{2,1,0:T(8,128)(2,1)} %copy.28), calls=%async_computation | async-start | bytes 4718592 | tf_op jit(solution)/shard_map/all_to_all | solution.py:392
  18.7 140.8 %all-gather.2.cloned.1.call-start = ((), (), s32[]{:S(2)}) async-start(), calls=%async_computation.2 | async-start | bytes 9289728 | tf_op jit(solution)/shard_map/all_gather | solution.py:405
  19.4 32.9 %copy-start.10 = (s32[4]{0:T(128)S(1)}, s32[4]{0:T(128)}, u32[]{:S(2)}) copy-start(s32[4]{0:T(128)} %param.15) | copy-start | bytes 52
  51.6 223.9 %reduce-scatter.2.cloned.1.call-start = ((), (), s32[]{:S(2)}) async-start(), calls=%async_computation.3 | async-start | bytes 5849088 | tf_op jit(solution)/shard_map/reduce_scatter | solution.py:469
  168.6 5.6 %copy-start.2 = (bf16[256,5376]{1,0:T(8,128)(2,1)S(1)}, bf16[256,5376]{1,0:T(8,128)(2,1)}, u32[]{:S(2)}) copy-start(bf16[256,5376]{1,0:T(8,128)(2,1)} %param.12) | copy-start | bytes 8257540
  168.6 5.6 %copy-start.9 = (f32[5376]{0:T(1024)S(1)}, f32[5376]{0:T(1024)}, u32[]{:S(2)}) copy-start(f32[5376]{0:T(1024)} %param.16) | copy-start | bytes 64516
  174.2 3.2 copy-start.1
  174.2 3.5 copy-start.6
  174.2 13.5 %copy-start.7 = (f32[128]{0:T(128)S(1)}, f32[128]{0:T(128)}, u32[]{:S(2)}) copy-start(f32[128]{0:T(128)} %param.17) | copy-start | bytes 1540
  178.4 9.6 %collective-permute-start = (bf16[2,1,256,128]{3,2,1,0:T(8,128)(2,1)S(1)}, bf16[2,1,256,128]{3,2,1,0:T(8,128)(2,1)S(1)}, u32[]{:S(2)}, u32[]{:S(2)}) collective-permute-start(bf16[2,1,256,128]{3,2,1,0:T(8,128)(2,1)S(1)} %pad_maximum_fusion), channel_id=1, source_target_pairs={{0,64},{16,80},{32,96},{48,112},{1,65},{17,81},{33,97},{49,113},{2... | collective-permute-start | bytes 393224 | tf_op jit(solution)/shard_map/ppermute | solution.py:333
  180.6 7.4 %collective-permute-start.1 = (bf16[2,1,256,128]{3,2,1,0:T(8,128)(2,1)S(1)}, bf16[2,1,256,128]{3,2,1,0:T(8,128)(2,1)S(1)}, u32[]{:S(2)}, u32[]{:S(2)}) collective-permute-start(bf16[2,1,256,128]{3,2,1,0:T(8,128)(2,1)S(1)} %pad_maximum_fusion), channel_id=1, source_target_pairs={{0,48},{16,64},{32,80},{48,96},{64,112},{1,49},{17,65},{33,81},{49... | collective-permute-start | bytes 393224 | tf_op jit(solution)/shard_map/ppermute | solution.py:333
  183.0 5.1 %collective-permute-start.2 = (bf16[2,1,256,128]{3,2,1,0:T(8,128)(2,1)S(1)}, bf16[2,1,256,128]{3,2,1,0:T(8,128)(2,1)S(1)}, u32[]{:S(2)}, u32[]{:S(2)}) collective-permute-start(bf16[2,1,256,128]{3,2,1,0:T(8,128)(2,1)S(1)} %pad_maximum_fusion), channel_id=1, source_target_pairs={{0,32},{16,48},{32,64},{48,80},{64,96},{80,112},{1,33},{17,49},{33... | collective-permute-start | bytes 393224 | tf_op jit(solution)/shard_map/ppermute | solution.py:333
  185.2 5.1 %collective-permute-start.3 = (bf16[2,1,256,128]{3,2,1,0:T(8,128)(2,1)S(1)}, bf16[2,1,256,128]{3,2,1,0:T(8,128)(2,1)S(1)}, u32[]{:S(2)}, u32[]{:S(2)}) collective-permute-start(bf16[2,1,256,128]{3,2,1,0:T(8,128)(2,1)S(1)} %pad_maximum_fusion), channel_id=1, source_target_pairs={{0,16},{16,32},{32,48},{48,64},{64,80},{80,96},{96,112},{1,17},{17... | collective-permute-start | bytes 393224 | tf_op jit(solution)/shard_map/ppermute | solution.py:333
  201.3 0.7 copy-start.5
  201.3 75.4 %copy-start.3 = (f32[5376]{0:T(1024)S(1)}, f32[5376]{0:T(1024)}, u32[]{:S(2)}) copy-start(f32[5376]{0:T(1024)} %param.19) | copy-start | bytes 64516
  201.3 76.6 %copy-start.4 = (f32[5376]{0:T(1024)S(1)}, f32[5376]{0:T(1024)}, u32[]{:S(2)}) copy-start(f32[5376]{0:T(1024)} %param.20) | copy-start | bytes 64516
  279.8 91.3 %copy-start.8 = (f32[16]{0:T(128)S(1)}, f32[16]{0:T(128)}, u32[]{:S(2)}) copy-start(f32[16]{0:T(128)} %param.23) | copy-start | bytes 196
Sparse Core Ops, SparseCore 0:
  51.8 107.7 all-gather.1
  201.5 74.0 reduce-scatter.1

commit v2 on v1

--- a/solution.py
+++ b/solution.py
@@ -327,32 +327,422 @@
     )(fin, table, actions.reshape(128, rows, 1))
 
 
-def from_behind(value, axis, steps):
-    count = lax.axis_size(axis)
-    leading, last = (max(0, -steps), min(count, count - steps))
-    return lax.ppermute(value, axis, [(source, source + steps) for source in range(leading, last)])
-
-
-def rms_scale(values, gain_vec):
-    mean_sq = jnp.mean(values * values, axis=-1, keepdims=True)
-    return values * lax.rsqrt(mean_sq + epsilon) * gain_vec
-
-
-def rotate(values, position):
-    half_size = values.shape[-1] // 2
-    frequency = rope_base ** (-2.0 * jnp.arange(half_size, dtype=jnp.float32) / values.shape[-1])
+A_COLS = 512
+
+
+def layer_kernel(
+    send_slot, keep_from, row_of, slot_of,
+    residual_ref, stored_ref, cos_ref, sin_ref, start_ref,
+    in_gain, q_gain, k_gain, post_gain, final_gain, out_ref,
+    out_a, out_b, in_a, in_b, held_a, held_b, cols, proj, kv, query, mixed, wout,
+    half_out, half_in, part_out, part_in, summed,
+    xa_s, xa_r, xb_s, xb_r,
+    ya_s, ya_r, za_s, za_r, fa_s, fa_r,
+    yb_s, yb_r, zb_s, zb_r, fb_s, fb_r,
+    h_s, h_r, c_s, c_r, p_s, p_r,
+):
+    ctx = lax.axis_index("ctx")
+    tp = lax.axis_index("tp")
+    core = tp % 2
+    chip = tp // 2
+    y_hi, z = ctx // 4, ctx % 4
+    n_blk = stored_ref.shape[0]
+    blk_rows = stored_ref.shape[1]
+    tokens, depth = residual_ref.shape
+    head = q_gain.shape[1]
+
+    def send(src, dst, send_sem, recv_sem, peer):
+        return pltpu.make_async_remote_copy(
+            src_ref=src, dst_ref=dst, send_sem=send_sem, recv_sem=recv_sem,
+            device_id=peer, device_id_type=MESH,
+        )
+
+    t_peer = lambda off: (ctx, (tp + off) % 16)
+    z_peer = lambda step: (y_hi * 4 + (z + step) % 4, tp)
+    y_peer = ((ctx + 4) % 8, tp)
+
+    def swap(out, got, ss, rs, off):
+        return send(out.at[(tp + off) % 16], got.at[tp], ss.at[off], rs.at[off], t_peer(off))
+
+    def stage(t, carry):
+        block = stored_ref[send_slot[t]]
+        out_a[t] = block[:, :A_COLS]
+        out_b[t] = block[:, A_COLS:]
+        return carry
+
+    lax.fori_loop(0, 16, stage, 0)
+    greet([((ctx + o) % 8, tp) for o in range(1, 8)] + [t_peer(o) for o in range(1, 16)])
+
+    def start_a(off, carry):
+        swap(out_a, in_a, xa_s, xa_r, off).start()
+        return carry
+
+    lax.fori_loop(1, 16, start_a, 0)
+    in_a[tp] = out_a[tp]
+    in_b[tp] = out_b[tp]
+
+    step_rows = 32
+
+    def norm_rows(i, carry):
+        at = pl.ds(pl.multiple_of(i * step_rows, step_rows), step_rows)
+        x = residual_ref[at].astype(jnp.float32)
+        scale = lax.rsqrt(jnp.mean(x * x, axis=-1, keepdims=True) + epsilon)
+        n = (x * scale * in_gain[...]).astype(jnp.bfloat16)
+        for r in range(depth // blk_rows):
+            cols[r, at, :blk_rows] = n[:, r * blk_rows:(r + 1) * blk_rows]
+        return carry
+
+    lax.fori_loop(0, tokens // step_rows, norm_rows, 0)
+    proj[...] = jnp.zeros_like(proj)
+
+    class Gather:
+        def __init__(self, held, got, ys, yr, zs, zr, fs, fr):
+            self.held, self.got = held, got
+            self.ys, self.yr, self.zs, self.zr, self.fs, self.fr = ys, yr, zs, zr, fs, fr
+
+        def y(self, k):
+            return send(self.held.at[0, 0, k], self.held.at[1, 0, k], self.ys.at[k], self.yr.at[k], y_peer)
+
+        def z(self, yy, step, k):
+            i = 0 if step == 1 else 1
+            return send(
+                self.held.at[yy, 0, k], self.held.at[yy, (4 - step) % 4, k],
+                self.zs.at[yy, i, k], self.zr.at[yy, i, k], z_peer(step),
+            )
+
+        def f(self, yy, step, k):
+            return send(
+                self.held.at[yy, 3 if step == 1 else 1, k], self.held.at[yy, 2, k],
+                self.fs.at[yy, k], self.fr.at[yy, k], z_peer(step),
+            )
+
+        def own(self, k):
+            self.held[0, 0, k] = self.got[keep_from[k]]
+            self.y(k).start()
+            self.z(0, 1, k).start()
+            self.z(0, 3, k).start()
+
+        def partner(self, k):
+            self.y(k).wait_recv()
+            self.z(1, 1, k).start()
+            self.z(1, 3, k).start()
+
+        def side(self, yy, k):
+            right = k < 4 - yy
+            self.z(yy, 1, k).wait_recv()
+
+            @pl.when(right)
+            def _():
+                self.f(yy, 1, k).start()
+
+            self.z(yy, 3, k).wait_recv()
+
+            @pl.when(jnp.logical_not(right))
+            def _():
+                self.f(yy, 3, k).start()
+
+        def far(self, yy, k):
+            self.f(yy, 1, k).wait_recv()
+
+        def sent(self, k):
+            self.y(k).wait_send()
+            for yy in range(2):
+                self.z(yy, 1, k).wait_send()
+                self.z(yy, 3, k).wait_send()
+                self.f(yy, 1, k).wait_send()
+
+    ga = Gather(held_a, in_a, ya_s, ya_r, za_s, za_r, fa_s, fa_r)
+    gb = Gather(held_b, in_b, yb_s, yb_r, zb_s, zb_r, fb_s, fb_r)
+
+    def term(yy, zz, k):
+        c = (y_hi + yy) % 2 * 4 + (z + zz) % 4
+        r = row_of[c * n_blk + k]
+        proj[...] += jnp.dot(
+            cols[r, :, :blk_rows], held_a[yy, zz, k], preferred_element_type=jnp.float32
+        )
+
+    def each_block(body):
+        def run(k, carry):
+            body(k)
+            return carry
+
+        lax.fori_loop(0, n_blk, run, 0)
+
+    def wait_a(off, carry):
+        swap(out_a, in_a, xa_s, xa_r, off).wait_recv()
+        return carry
+
+    lax.fori_loop(1, 16, wait_a, 0)
+    each_block(ga.own)
+
+    def start_b(off, carry):
+        swap(out_b, in_b, xb_s, xb_r, off).start()
+        return carry
+
+    lax.fori_loop(1, 16, start_b, 0)
+
+    def one(k):
+        ga.partner(k)
+        term(0, 0, k)
+
+    def two(k):
+        ga.side(0, k)
+        term(0, 3, k)
+        term(0, 1, k)
+
+    def three(k):
+        ga.side(1, k)
+        term(1, 0, k)
+        term(1, 3, k)
+        term(1, 1, k)
+
+    def four(yy):
+        def run(k):
+            ga.far(yy, k)
+            term(yy, 2, k)
+
+        return run
+
+    each_block(one)
+    each_block(two)
+    each_block(three)
+
+    def wait_b(off, carry):
+        swap(out_b, in_b, xb_s, xb_r, off).wait_recv()
+        return carry
+
+    lax.fori_loop(1, 16, wait_b, 0)
+    each_block(gb.own)
+    each_block(four(0))
+    each_block(gb.partner)
+    each_block(four(1))
+
+    def heads(at, gain):
+        e = proj[:, pl.ds(at * head, head)]
+        scale = lax.rsqrt(jnp.mean(e * e, axis=-1, keepdims=True) + epsilon)
+        e = e * scale * gain[...]
+        return (e * cos_ref[...] + pltpu.roll(e, head // 2, 1) * sin_ref[...]).astype(jnp.bfloat16)
+
+    reach = kv.shape[0] - 1
+    kv[reach, :, :head] = heads(2, k_gain)
+    kv[reach, :, head:] = proj[:, 3 * head:].astype(jnp.bfloat16)
+
+    def halo(step):
+        return send(
+            kv.at[reach], kv.at[reach - step], h_s.at[step - 1], h_r.at[step - 1],
+            ((ctx + step) % 8, tp),
+        )
+
+    for step in range(1, reach + 1):
+        @pl.when(ctx + step < 8)
+        def _():
+            halo(step).start()
+
+        @pl.when(ctx < step)
+        def _():
+            kv[reach - step] = jnp.zeros(kv.shape[1:], kv.dtype)
+
+    for h in range(2):
+        query[h] = heads(h, q_gain)
+    for yy in range(2):
+        each_block(lambda k: gb.side(yy, k))
+    for step in range(1, reach + 1):
+        @pl.when(ctx >= step)
+        def _():
+            halo(step).wait_recv()
+
+    span = (reach + 1) * tokens
+    key_rows = kv[:, :, :head].reshape(span, head)
+    value_rows = kv[:, :, head:].reshape(span, head)
+    q_ids = ctx * tokens + lax.broadcasted_iota(jnp.int32, (tokens, span), 0)
+    k_ids = (ctx - reach) * tokens + lax.broadcasted_iota(jnp.int32, (tokens, span), 1)
+    visible = (k_ids <= q_ids) & (q_ids - k_ids < WINDOW) & (k_ids >= start_ref[...])
+    for h in range(2):
+        scores = lax.dot_general(
+            query[h], key_rows, (((1,), (1,)), ((), ())), preferred_element_type=jnp.float32
+        ) * QUERY_SCALAR ** (-0.5)
+        probs = jnp.where(visible, jnp.exp(scores), 0.0)
+        probs = (probs / jnp.sum(probs, axis=1, keepdims=True)).astype(jnp.bfloat16)
+        got = jnp.dot(probs, value_rows, preferred_element_type=jnp.float32).astype(jnp.bfloat16)
+        mixed[:, :, :, h * head:(h + 1) * head] = got.reshape(8, 2, tokens // 16, head)
+
+    for yy in range(2):
+        each_block(lambda k: gb.far(yy, k))
+
+    def order(r, carry):
+        wout[r] = held_b.reshape(8 * n_blk, blk_rows, 2 * head)[slot_of[r]]
+        return carry
+
+    lax.fori_loop(0, depth // blk_rows, order, 0)
+
+    share = tokens // 16
+    per = wout.shape[0] // half_out.shape[0]
+    piece = per * blk_rows
+    other = (tp // 2) * 2 + (1 - core)
+
+    def product(which, n):
+        rows = mixed[:, which].reshape(8 * share, 2 * head)
+        block = wout[pl.ds(n * per, per)].reshape(piece, 2 * head)
+        return lax.dot_general(
+            rows, block, (((1,), (1,)), ((), ())), preferred_element_type=jnp.float32
+        ).reshape(8, share, piece)
+
+    def between(n):
+        return send(half_out.at[n], half_in.at[n], c_s.at[n], c_r.at[n], (ctx, other))
+
+    def to_chip(n, off):
+        there = (chip + off) % 8
+        return send(
+            part_out.at[n, there], part_in.at[n, off], p_s.at[n, off], p_r.at[n, off],
+            (ctx, there * 2 + core),
+        )
+
+    n_pieces = half_out.shape[0]
+
+    def give(n, carry):
+        half_out[n] = product(1 - core, n).astype(jnp.bfloat16)
+        between(n).start()
+        return carry
+
+    def take(n, carry):
+        mine = product(core, n)
+        between(n).wait_recv()
+        part_out[n] = (mine + half_in[n].astype(jnp.float32)).astype(jnp.bfloat16)
+        for off in range(1, 8):
+            to_chip(n, off).start()
+        return carry
+
+    lax.fori_loop(0, n_pieces, give, 0)
+    lax.fori_loop(0, n_pieces, take, 0)
+    for n in range(n_pieces):
+        total = part_out[n, chip].astype(jnp.float32)
+        for off in range(1, 8):
+            to_chip(n, off).wait_recv()
+            total = total + part_in[n, off].astype(jnp.float32)
+        summed[:, n * piece:(n + 1) * piece] = total
+
+    def rms(values, gain):
+        return values * lax.rsqrt(jnp.mean(values * values, axis=-1, keepdims=True) + epsilon) * gain[...]
+
+    mine = residual_ref[pl.ds(pl.multiple_of(tp * share, share), share)].astype(jnp.float32)
+    hidden = mine + rms(summed[...], post_gain)
+    out_ref[...] = rms(hidden, final_gain).astype(jnp.bfloat16)
+
+    def swapped(off, carry):
+        swap(out_a, in_a, xa_s, xa_r, off).wait_send()
+        swap(out_b, in_b, xb_s, xb_r, off).wait_send()
+        return carry
+
+    lax.fori_loop(1, 16, swapped, 0)
+    each_block(ga.sent)
+    each_block(gb.sent)
+    for step in range(1, reach + 1):
+        @pl.when(ctx + step < 8)
+        def _():
+            halo(step).wait_send()
+
+    def parts_sent(n, carry):
+        between(n).wait_send()
+        for off in range(1, 8):
+            to_chip(n, off).wait_send()
+        return carry
+
+    lax.fori_loop(0, n_pieces, parts_sent, 0)
+
+
+def layer(
+    send_slot, keep_from, row_of, slot_of, residual, stored, cosine, sine, seg_start,
+    in_gain, q_gain, k_gain, post_gain, final_gain,
+):
+    tokens, depth = residual.shape
+    n_blk, blk_rows, width = stored.shape
+    head = q_gain.shape[0]
+    share = tokens // 16
+    bf16 = jnp.bfloat16
+    n_rows = depth // blk_rows
+    n_pieces = 7
+    piece = depth // n_pieces
+    reach = WINDOW // tokens
+    dma = pltpu.SemaphoreType.DMA
+    b_cols = width - A_COLS
+    smem = pl.BlockSpec(memory_space=pltpu.SMEM)
+    vmem = pl.BlockSpec(memory_space=VMEM)
+    gather_sems = [dma((n_blk,))] * 2 + [dma((2, 2, n_blk))] * 2 + [dma((2, n_blk))] * 2
+    return pl.pallas_call(
+        layer_kernel,
+        out_shape=jax.ShapeDtypeStruct((share, depth), bf16),
+        in_specs=[smem] * 4 + [vmem] * 10,
+        out_specs=vmem,
+        scratch_shapes=[
+            VMEM((16, blk_rows, A_COLS), bf16),
+            VMEM((16, blk_rows, b_cols), bf16),
+            VMEM((16, blk_rows, A_COLS), bf16),
+            VMEM((16, blk_rows, b_cols), bf16),
+            VMEM((2, 4, n_blk, blk_rows, A_COLS), bf16),
+            VMEM((2, 4, n_blk, blk_rows, b_cols), bf16),
+            VMEM((n_rows, tokens, 128), bf16),
+            VMEM((tokens, A_COLS), jnp.float32),
+            VMEM((reach + 1, tokens, 2 * head), bf16),
+            VMEM((2, tokens, head), bf16),
+            VMEM((8, 2, share, 2 * head), bf16),
+            VMEM((n_rows, blk_rows, b_cols), bf16),
+            VMEM((n_pieces, 8, share, piece), bf16),
+            VMEM((n_pieces, 8, share, piece), bf16),
+            VMEM((n_pieces, 8, share, piece), bf16),
+            VMEM((n_pieces, 8, share, piece), bf16),
+            VMEM((share, depth), jnp.float32),
+        ]
+        + [dma((16,))] * 4
+        + gather_sems * 2
+        + [dma((reach,))] * 2
+        + [dma((n_pieces,))] * 2
+        + [dma((n_pieces, 8))] * 2,
+        compiler_params=pltpu.CompilerParams(
+            collective_id=1, has_side_effects=True, vmem_limit_bytes=60 * 2**20
+        ),
+        name="layer",
+    )(
+        send_slot, keep_from, row_of, slot_of, residual, stored, cosine, sine, seg_start[:, None],
+        in_gain[None], q_gain[None], k_gain[None], post_gain[None], final_gain[None],
+    )
+
+
+def rope_tables(position, head):
+    half_size = head // 2
+    frequency = rope_base ** (-2.0 * jnp.arange(half_size, dtype=jnp.float32) / head)
     angle_rows = position.astype(jnp.float32)[:, None] * frequency[None, :]
-    cosine = jnp.cos(angle_rows)
-    sine_part = jnp.sin(angle_rows)
-    first_half = values[..., :half_size]
-    second_half = values[..., half_size:]
-    return jnp.concatenate(
-        [
-            first_half * cosine - second_half * sine_part,
-            second_half * cosine + first_half * sine_part,
-        ],
-        axis=-1,
+    cosine, sine = jnp.cos(angle_rows), jnp.sin(angle_rows)
+    return (
+        jnp.concatenate([cosine, cosine], axis=-1),
+        jnp.concatenate([-sine, sine], axis=-1),
     )
+
+
+def block_tables(block_list, ctx_index, tp_index, ctx_count, tp_count, blocks_dev):
+    rows_per_reader = blocks_dev * ctx_count
+    grid = block_list.reshape(ctx_count, tp_count, blocks_dev)
+    readers = grid // rows_per_reader
+    my_readers = lax.dynamic_slice(
+        readers, (ctx_index, tp_index, 0), (1, 1, blocks_dev)
+    ).reshape(-1)
+    slots = jnp.arange(blocks_dev, dtype=jnp.int32)
+    sources = jnp.arange(tp_count, dtype=jnp.int32)
+    send_slot = jnp.sum(jnp.where(my_readers[None, :] == sources[:, None], slots[None, :], 0), axis=1)
+    hit = readers == tp_index
+    present = jnp.any(hit, axis=2)
+    row_index = jnp.sum(jnp.where(hit, grid % rows_per_reader, 0), axis=2)
+    before = sources[None, :] < sources[:, None]
+    rank = jnp.sum((present[:, None, :] & before[None]).astype(jnp.int32), axis=2)
+    chosen = (rank[:, None, :] == slots[None, :, None]) & present[:, None, :]
+    row_of = jnp.sum(jnp.where(chosen, row_index[:, None, :], 0), axis=2)
+    keep_all = jnp.sum(jnp.where(chosen, sources[None, None, :], 0), axis=2)
+    keep_from = lax.dynamic_index_in_dim(keep_all, ctx_index, 0, False)
+    ids = jnp.arange(ctx_count, dtype=jnp.int32)
+    side = (ids // 4 + ctx_index // 4) % 2
+    slot = (side * 4 + (ids + 4 - ctx_index % 4) % 4)[:, None] * blocks_dev + slots[None, :]
+    rows = jnp.arange(rows_per_reader, dtype=jnp.int32)
+    slot_of = jnp.sum(jnp.where(row_of.reshape(1, -1) == rows[:, None], slot.reshape(1, -1), 0), axis=1)
+    return send_slot, keep_from, row_of.reshape(-1), slot_of
 
 
 def shards(
@@ -374,109 +764,20 @@
     ctx_index = lax.axis_index("ctx")
     tp_index = lax.axis_index("tp")
     row_count = residual.shape[0]
-    blocks_dev = stored_blocks.shape[0]
-    rows_per_reader = blocks_dev * ctx_count
-    list_grid = block_list.reshape(ctx_count, tp_count, blocks_dev)
-    reader_ids = list_grid // rows_per_reader
-    row_index_all = list_grid % rows_per_reader
-    my_list = lax.dynamic_index_in_dim(
-        lax.dynamic_index_in_dim(list_grid, ctx_index, 0, False), tp_index, 0, False
+    share_rows = row_count // tp_count
+    tables = block_tables(
+        block_list, ctx_index, tp_index, ctx_count, tp_count, stored_blocks.shape[0]
     )
-    my_readers = my_list // rows_per_reader
-    send_mask = (my_readers[None, :] == jnp.arange(tp_count, dtype=jnp.int32)[:, None]).astype(
-        jnp.bfloat16
-    )
-    outgoing = jnp.einsum(
-        "tk,krc->trc", send_mask, stored_blocks, preferred_element_type=jnp.float32
-    ).astype(jnp.bfloat16)
-    incoming = lax.all_to_all(outgoing, "tp", split_axis=0, concat_axis=0, tiled=True)
-    reader_hit = reader_ids == tp_index
-    present = jnp.any(reader_hit, axis=2).astype(jnp.int32)
-    row_index = jnp.sum(jnp.where(reader_hit, row_index_all, 0), axis=2)
-    rank_ids = jnp.cumsum(present, axis=1) - 1
-    choose_mask = (
-        rank_ids[:, None, :] == jnp.arange(blocks_dev, dtype=jnp.int32)[None, :, None]
-    ) & (present[:, None, :] == 1)
-    kept_index = jnp.sum(jnp.where(choose_mask, row_index[:, None, :], 0), axis=2).reshape(-1)
-    my_choose = lax.dynamic_index_in_dim(choose_mask, ctx_index, 0, False).astype(jnp.bfloat16)
-    kept_blocks = jnp.einsum(
-        "ks,src->krc", my_choose, incoming, preferred_element_type=jnp.float32
-    ).astype(jnp.bfloat16)
-    gathered = lax.all_gather(kept_blocks, "ctx", axis=0, tiled=True)
-    slot_ids = jnp.arange(kept_index.shape[0], dtype=jnp.int32)
-    placement = jnp.sum(
-        jnp.where(
-            kept_index[None, :] == jnp.arange(rows_per_reader, dtype=jnp.int32)[:, None],
-            slot_ids[None, :],
-            0,
-        ),
-        axis=1,
-    )
-    reader_weight = jnp.take(gathered, placement, axis=0).reshape(residual.shape[1], -1)
-    query_width = HEADS // tp_count * HEAD_DIM
-    key_width = KV_HEADS // tp_count * HEAD_DIM
-    group_size = HEADS // KV_HEADS
     seq_starts = jnp.cumsum(lengths) - lengths
     query_ids = ctx_index * row_count + jnp.arange(row_count, dtype=jnp.int32)
     seg_start = jnp.max(
         jnp.where(seq_starts[None, :] <= query_ids[:, None], seq_starts[None, :], 0), axis=1
     )
-    position = query_ids - seg_start
-    normed = rms_scale(residual.astype(jnp.float32), in_gain).astype(jnp.bfloat16)
-    projected = jnp.dot(
-        normed, reader_weight[:, : query_width + 2 * key_width], preferred_element_type=jnp.float32
+    cosine, sine = rope_tables(query_ids - seg_start, HEAD_DIM)
+    final = layer(
+        *tables, residual, stored_blocks, cosine, sine, seg_start,
+        in_gain, q_gain, k_gain, post_gain, final_gain,
     )
-    query_rows = projected[:, :query_width].reshape(row_count, -1, HEAD_DIM).transpose(1, 0, 2)
-    key_rows = (
-        projected[:, query_width : query_width + key_width]
-        .reshape(row_count, -1, HEAD_DIM)
-        .transpose(1, 0, 2)
-    )
-    value_rows = (
-        projected[:, query_width + key_width :].reshape(row_count, -1, HEAD_DIM).transpose(1, 0, 2)
-    )
-    query_rows = rotate(rms_scale(query_rows, q_gain), position).astype(jnp.bfloat16)
-    key_rows = rotate(rms_scale(key_rows, k_gain), position).astype(jnp.bfloat16)
-    key_value = jnp.stack([key_rows, value_rows.astype(jnp.bfloat16)])
-    reach_count = WINDOW // row_count
-    earlier = [from_behind(key_value, "ctx", step_back) for step_back in range(reach_count, 0, -1)]
-    before_rows = jnp.concatenate(earlier, axis=2)
-    window_kv = jnp.concatenate([before_rows, key_value], axis=2)
-    key_ids = (ctx_index - reach_count) * row_count + jnp.arange(
-        window_kv.shape[2], dtype=jnp.int32
-    )
-    visible = (
-        (key_ids[None, :] <= query_ids[:, None])
-        & (query_ids[:, None] - key_ids[None, :] < WINDOW)
-        & (key_ids[None, :] >= seg_start[:, None])
-    )
-    grouped = query_rows.reshape(-1, group_size, row_count, HEAD_DIM)
-    scores = jnp.einsum(
-        "hgqd,hkd->hgqk", grouped, window_kv[0], preferred_element_type=jnp.float32
-    ) * QUERY_SCALAR ** (-0.5)
-    prob_rows = jnp.where(visible, jnp.exp(scores), 0.0)
-    prob_rows = (prob_rows / jnp.sum(prob_rows, axis=3, keepdims=True)).astype(jnp.bfloat16)
-    mixed_out = jnp.einsum(
-        "hgqk,hkd->hgqd", prob_rows, window_kv[1], preferred_element_type=jnp.float32
-    ).astype(jnp.bfloat16)
-    mixed_flat = (
-        mixed_out.reshape(-1, row_count, HEAD_DIM)
-        .transpose(1, 0, 2)
-        .reshape(row_count, query_width)
-    )
-    out_columns = reader_weight[:, query_width + 2 * key_width :]
-    share_rows = row_count // tp_count
-    summed = lax.psum_scatter(
-        lax.dot_general(
-            mixed_flat, out_columns, (((1,), (1,)), ((), ())), preferred_element_type=jnp.float32
-        ),
-        "tp",
-        scatter_dimension=0,
-        tiled=True,
-    )
-    own_rows = lax.dynamic_slice_in_dim(residual, tp_index * share_rows, share_rows, 0)
-    hidden = own_rows.astype(jnp.float32) + rms_scale(summed, post_gain)
-    final = rms_scale(hidden, final_gain).astype(jnp.bfloat16)
     all_rows = vocab_stats(final, vocab_table, actions)
     ref_logprob = lax.dynamic_slice_in_dim(all_rows[0], tp_index * share_rows, share_rows, 0)
     return (ref_logprob, old_logprob - ref_logprob)

time: 379 us -> 241 us (0.64)
  waiting for transfers between devices: 207 us -> 0 us
  Pallas kernels: 90.6 us -> 223 us
  starting transfers between devices: 16.1 us -> 0 us
  matrix products: 15.2 us -> 0 us
  between operations: 14.4 us -> 0.73 us
  other arithmetic: 16.6 us -> 7.27 us
  local copies, waits for them, and re-layouts: 18.7 us -> 9.71 us
    pallas_call x0 -> x1, Pallas kernels: none -> 131 us  [layer(): pl.pallas_call(layer_kernel, out_shape=jax.ShapeDtypeStruct((share, depth...]
    all_gather x1 -> x0, waiting for transfers between devices: 104 us -> none  [shards(): gathered = lax.all_gather(kept_blocks, 'ctx', axis=0, tiled=True)]
    reduce_scatter x1 -> x0, waiting for transfers between devices: 71.6 us -> none  [shards(): lax.psum_scatter(lax.dot_general(mixed_flat, out_columns, (((1,), (1,)),...]
    all_to_all x1 -> x0, waiting for transfers between devices: 29.5 us -> none  [shards(): lax.all_to_all(outgoing, 'tp', split_axis=0, concat_axis=0, tiled=True)]
    dot_general x6 -> x0, matrix products: 15.2 us -> none  [the longest x1 5.17 us: shards(): lax.dot_general(mixed_flat, out_columns, (((1,), (1,)), ((), ())), prefer...]
    ppermute x4 -> x0, starting transfers between devices: 9.2 us -> none  [from_behind(): lax.ppermute(value, axis, [(source, source + steps) for source in range(l...]
    gather x1 -> x0, local copies, waits for them, and re-layouts: 9 us -> none  [shards(): jnp.take(gathered, placement, axis=0).reshape(residual.shape[1], -1)]
    all_to_all x1 -> x0, starting transfers between devices: 6.82 us -> none  [shards(): lax.all_to_all(outgoing, 'tp', split_axis=0, concat_axis=0, tiled=True)]
  transfers between devices with their start and end apart: 7 -> 0, of which waited for: 4 -> 0; matrix products, arithmetic and copies ran while one was open for 2% -> 0% of each run, Pallas kernels for 0% -> 0%
where the time goes in v2:
time: 241 us
  Pallas kernels  223 us (93%)
  local copies, waits for them, and re-layouts  9.71 us (4%)
  other arithmetic  7.27 us (3%)
    pallas_call x1, Pallas kernels, layer(): pl.pallas_call(layer_kernel, out_shape=jax.ShapeDtypeStruct((share, depth...  131 us
    pallas_call x1, Pallas kernels, vocab_stats(): pl.pallas_call(vocab_kernel, out_shape=jax.ShapeDtypeStruct((8, 16 * rows...  92 us

profile of v2, /device:TPU:1, one launch (start us, length us, event | category | flops | bytes accessed | tf_op | source)
XLA Modules:
  0.0 240.7 jit_solution(15551080734258149029)
XLA Ops:
  0.6 0.0 copy-start.1
  0.7 0.8 reduce-window.9
  1.5 0.7 bitcast_subtract_fusion
  2.2 0.7 sign_compare_fusion
  2.9 0.1 select_reduce_fusion.3
  3.0 0.1 iota_add_fusion
  3.1 0.1 add.116
  3.1 0.7 broadcast_remainder_fusion
  3.8 0.2 ne.88
  4.1 1.4 broadcast_in_dim.101.in_gain
  5.4 1.4 broadcast_in_dim.104.post_gain
  6.8 1.4 broadcast_in_dim.105.final_gain
  8.1 0.2 rem.75
  8.3 0.2 div.32
  8.5 0.2 fusion.14
  8.8 0.2 fusion.1
  9.0 0.6 select_reduce_fusion.4.send_slot
  9.6 0.2 convert_reduce_fusion
  9.8 0.3 select_reduce_fusion.1
  10.1 0.1 copy.19
  10.2 0.1 reshape.137.row_of
  10.3 0.7 select_reduce_fusion.slot_of
  11.0 0.7 dynamic-slice_reduce_fusion.keep_from
  11.7 0.8 copy.20.start_ref
  12.5 0.5 fusion.2
  13.0 0.8 pad_maximum_fusion
  13.8 131.0 %layer.1.fin_ref = bf16[16,5376]{1,0:T(8,128)(2,1)} custom-call(s32[16]{0:T(128)} %select_reduce_fusion.4.send_slot, s32[7]{0:T(128)} %dynamic-slice_reduce_fusion.keep_from, s32[56]{0:T(128)} %copy-done, s32[56]{0:T(128)} %select_reduce_fusion.slot_of, bf16[256,5376]{1,0:T(8,128)(2,1)} %residual_ref.1, bf16[7,96,768]{2,1,0:T(8,128)(2,1)} %stored_ref.1, ...), custom_call_target="tpu_custom_call" | custom-call | tf_op jit(solution)/shard_map/layer/pallas_call | solution.py:671
  144.8 2.6 %reshape.141.actions_ref = s32[128,16,1]{2,1,0:T(8,128)} reshape(s32[2048]{0:T(1024)} %param.22) | data formatting | bytes 16384 | tf_op jit(solution)/shard_map/reshape | solution.py:327
  147.4 92.0 %vocab_stats.1 = f32[8,256]{1,0:T(8,128)} custom-call(bf16[16,5376]{1,0:T(8,128)(2,1)} %layer.1.fin_ref, bf16[1152,5376]{1,0:T(8,128)(2,1)} %table_ref.1, s32[128,16,1]{2,1,0:T(8,128)} %reshape.141.actions_ref), custom_call_target="tpu_custom_call" | custom-call | tf_op jit(solution)/shard_map/vocab_stats/pallas_call | solution.py:295
  239.4 0.7 slice.3
  240.1 0.0 copy-done.1
  240.1 0.6 fusion.12
  (8 shorter events, 0.1 us)
Async XLA Ops:
  0.6 239.5 %copy-start.1 = (f32[16]{0:T(128)S(1)}, f32[16]{0:T(128)}, u32[]{:S(2)}) copy-start(f32[16]{0:T(128)} %param.23) | copy-start | bytes 196
  10.3 3.5 %copy-start = (s32[56]{0:T(128)}, s32[56]{0:T(128)S(1)}, u32[]{:S(2)}) copy-start(s32[56]{0:T(128)S(1)} %reshape.137.row_of) | copy-start | bytes 676

commit v3 on v2

--- a/solution.py
+++ b/solution.py
@@ -55,7 +55,7 @@
 
 def vocab_kernel(
     fin_ref, table_ref, actions_ref, out_ref,
-    buf, table, acc, part_exp, part_hit, st1, r1, st2, r2,
+    buf, table, acc, part_exp, part_hit, column, st1, r1, st2, r2,
     table_sem, s1, v1, s2, v2, s3, v3, sf, vf, sk, vk, sa, va, sb, vb,
 ):
     ctx = lax.axis_index("ctx")
@@ -140,15 +140,13 @@
     for p in range(3):
         own_chunk(p, 1)
 
-    def slab_of(g):
-        return jnp.where(g < 2, 0, jnp.where(g > 5, 2, jnp.where(g % 2 == 0, 3, 1)))
-
-    def half_of(g):
-        return jnp.where(g < 2, g, jnp.where(g > 5, g - 6, (g - 2) // 2))
+    def slab_of(g, i):
+        return jnp.where(g < 2, 0, jnp.where(g > 5, 2, 3 - 2 * i))
+
+    def row_of(g, i):
+        return jnp.where(g < 2, g * 2 + i, jnp.where(g > 5, (g - 6) * 2 + i, g - 2))
 
     def arrivals(g):
-        slab, half = slab_of(g), half_of(g)
-
         @pl.when(g == 1)
         def _():
             for q in (2, 3):
@@ -157,28 +155,27 @@
 
         @pl.when((g > 1) & (g < 6))
         def _():
-            for i in range(2):
-                q = half * 2 + i
-                for p in range(3):
-                    pltpu.make_async_remote_copy(
-                        src_ref=buf.at[p, 0, q, core], dst_ref=buf.at[p, slab, q, core],
-                        send_sem=s3.at[p, slab, q], recv_sem=v3.at[p, slab, q],
-                        device_id=sibling(), device_id_type=MESH,
-                    ).wait_recv()
-                    if i == 0:
-                        @pl.when(slab == 3)
-                        def _():
-                            passed(p, 3, q, 1).start()
-                    else:
-                        @pl.when(slab == 1)
-                        def _():
-                            passed(p, 1, q, 3).start()
-                    across(p, slab, q).start()
+            q = g - 2
+            for p in range(3):
+                third(p, q, 1).wait_recv()
+
+                @pl.when(q % 2 == 0)
+                def _():
+                    passed(p, 3, q, 1).start()
+
+                across(p, 3, q).start()
+                third(p, q, 3).wait_recv()
+
+                @pl.when(q % 2 == 1)
+                def _():
+                    passed(p, 1, q, 3).start()
+
+                across(p, 1, q).start()
 
         @pl.when((g > 5) & (g < 8))
         def _():
             for i in range(2):
-                q = half * 2 + i
+                q = (g - 6) * 2 + i
                 for p in range(3):
                     passed(p, 3, q, 1).wait_recv()
                     across(p, 2, q).start()
@@ -187,35 +184,80 @@
         x, y, z = axis_values
         return ((y // 2) * 4 + z) * 16 + x * 4 + (y % 2) * 2 + k
 
+    first_id = (ctx * 16 + tp) * vocab_rows
+    ids = first_id + lax.broadcasted_iota(jnp.int32, (rows, vocab_rows), 1)
+
+    def fold(v):
+        total = v[:, :128]
+        for i in range(1, vocab_rows // 128):
+            total = total + v[:, i * 128:(i + 1) * 128]
+        return total
+
+    def tail(rel):
+        at = place([(own[i] + rel[i]) % 4 for i in range(3)], 0)
+        for kk in range(2):
+            capped = soft_cap * jnp.tanh(acc[at + kk] * (1.0 / soft_cap))
+            hit = ids == column[at + kk]
+            part_exp[at + kk] = fold(jnp.exp(capped))
+            part_hit[at + kk] = fold(jnp.where(hit, capped, 0.0))
+
+    def near(digit):
+        return digit + digit // 2
+
+    def early_tail(i, carry):
+        for j in range(3):
+            tail((near(i // 3), near(i % 3), near(j)))
+        return carry
+
+    def late_x(i, carry):
+        for j in range(4):
+            tail((2, i, j))
+        return carry
+
+    def late_y(i, carry):
+        for j in range(4):
+            tail((near(i), 2, j))
+        return carry
+
+    def late_z(i, carry):
+        for j in range(3):
+            tail((near(i), near(j), 2))
+        return carry
+
     def group(g, carry):
-        slab, half = slab_of(g), half_of(g)
+        slabs, lines = [slab_of(g, i) for i in range(2)], [row_of(g, i) for i in range(2)]
         for p in range(3):
             for i in range(2):
-                across(p, slab, half * 2 + i).wait_recv()
+                across(p, slabs[i], lines[i]).wait_recv()
 
             @pl.when(g == 0)
             def _():
                 table_copy(p).wait()
 
-            lhs = buf[p, slab, pl.ds(half * 2, 2)].reshape(16 * rows, width)
+            lhs = jnp.concatenate(
+                [buf[p, slabs[i], lines[i]].reshape(8 * rows, width) for i in range(2)], axis=0
+            )
             got = lax.dot_general(
                 lhs, table[p], (((1,), (1,)), ((), ())), preferred_element_type=jnp.float32
             )
             a1, a2, a3 = (axis_of(p, i) for i in range(3))
             for i in range(2):
-                q = half * 2 + i
-                rel2 = jnp.where(q < 2, q, 5 - q)
+                rel2 = jnp.where(lines[i] < 2, lines[i], 5 - lines[i])
                 for kk in range(2):
                     for r1_ in range(4):
                         at = [None] * 3
                         at[a1] = (own[a1] + r1_) % 4
                         at[a2] = (own[a2] + rel2) % 4
-                        at[a3] = (own[a3] + slab) % 4
+                        at[a3] = (own[a3] + slabs[i]) % 4
                         d = place(at, kk)
                         m = (i * 2 + kk) * 4 + r1_
                         value = got[m * rows:(m + 1) * rows]
                         acc[d] = acc[d] + value
             if p == 0:
+                @pl.when(g == 6)
+                def _():
+                    lax.fori_loop(0, 9, early_tail, 0)
+
                 arrivals(g + 1)
         return carry
 
@@ -224,33 +266,34 @@
         return carry
 
     lax.fori_loop(0, 128, clear, 0)
+    lanes = lax.broadcasted_iota(jnp.int32, (128, 128), 1)
+    diagonal = lax.broadcasted_iota(jnp.int32, (128, 128), 0) == lanes
+
+    def turn(j, carry):
+        line = jnp.broadcast_to(actions_ref[pl.ds(j, 1)].astype(jnp.float32), (128, 128))
+        turned = jnp.sum(jnp.where(diagonal, line, 0.0), axis=1, keepdims=True)
+        column[pl.ds(j * 8, 8)] = turned.astype(jnp.int32).reshape(8, rows, 1)
+        return carry
+
+    lax.fori_loop(0, actions_ref.shape[0], turn, 0)
     lax.fori_loop(0, 8, group, 0)
 
-    first_id = (ctx * 16 + tp) * vocab_rows
-    ids = first_id + lax.broadcasted_iota(jnp.int32, (rows, vocab_rows), 1)
-
-    def fold(v):
-        total = v[:, :128]
-        for i in range(1, vocab_rows // 128):
-            total = total + v[:, i * 128:(i + 1) * 128]
-        return total
-
-    def tail(d, carry):
-        capped = soft_cap * jnp.tanh(acc[d] * (1.0 / soft_cap))
-        hit = ids == actions_ref[d]
-        part_exp[d] = fold(jnp.exp(capped))
-        part_hit[d] = fold(jnp.where(hit, capped, 0.0))
-        return carry
-
-    lax.fori_loop(0, 128, tail, 0)
+    lax.fori_loop(0, 4, late_x, 0)
+    lax.fori_loop(0, 3, late_y, 0)
+    lax.fori_loop(0, 3, late_z, 0)
     ones = jnp.ones((8, 128), jnp.float32)
     for c in range(8):
-        for row, part in ((0, part_exp), (1, part_hit)):
-            got = lax.dot_general(
+        sums = [
+            lax.dot_general(
                 ones, part[pl.ds(c * 16, 16)].reshape(16 * rows, 128), (((1,), (1,)), ((), ())),
                 preferred_element_type=jnp.float32, precision=lax.Precision.HIGHEST,
             )
-            st1[c, row * 8:(row + 1) * 8, :] = got
+            for part in (part_exp, part_hit)
+        ]
+        st1[c] = jnp.concatenate(
+            [v[:1, i * 128:(i + 1) * 128] for v in (sums + sums) for i in range(2)], axis=0
+        )
+
     def stage1(off):
         return send(st1.at[(ctx + off) % 8], r1.at[off], sa.at[off], va.at[off], c_peer(off))
 
@@ -269,7 +312,7 @@
     for off in range(1, 16):
         stage2(off).wait_recv()
         total = total + r2[off]
-    out_ref[...] = total[8:] - jnp.log(total[:8])
+    out_ref[...] = total[2:4] - jnp.log(total[:2])
 
     for p in range(3):
         for step in (1, 2, 3):
@@ -294,7 +337,7 @@
     dma = pltpu.SemaphoreType.DMA
     return pl.pallas_call(
         vocab_kernel,
-        out_shape=jax.ShapeDtypeStruct((8, 16 * rows), jnp.float32),
+        out_shape=jax.ShapeDtypeStruct((2, 128), jnp.float32),
         in_specs=[
             pl.BlockSpec(memory_space=VMEM),
             pl.BlockSpec(memory_space=pl.ANY),
@@ -307,10 +350,11 @@
             VMEM((128, rows, vocab_rows), jnp.float32),
             VMEM((128, rows, 128), jnp.float32),
             VMEM((128, rows, 128), jnp.float32),
-            VMEM((8, 16, 16 * rows), jnp.float32),
-            VMEM((8, 16, 16 * rows), jnp.float32),
-            VMEM((16, 16 * rows), jnp.float32),
-            VMEM((16, 16, 16 * rows), jnp.float32),
+            VMEM((128, rows, 1), jnp.int32),
+            VMEM((8, 8, 128), jnp.float32),
+            VMEM((8, 8, 128), jnp.float32),
+            VMEM((8, 128), jnp.float32),
+            VMEM((16, 8, 128), jnp.float32),
             dma((3,)),
             dma((3, 3)), dma((3, 3)),
             dma((3, 4)), dma((3, 4)),
@@ -324,7 +368,7 @@
             collective_id=2, has_side_effects=True, vmem_limit_bytes=60 * 2**20
         ),
         name="vocab_stats",
-    )(fin, table, actions.reshape(128, rows, 1))
+    )(fin, table, actions.reshape(-1, 128))
 
 
 A_COLS = 512
@@ -332,8 +376,8 @@
 
 def layer_kernel(
     send_slot, keep_from, row_of, slot_of,
-    residual_ref, stored_ref, cos_ref, sin_ref, start_ref,
-    in_gain, q_gain, k_gain, post_gain, final_gain, out_ref,
+    lengths, residual_ref, stored_ref, frequency, in_lines, post_lines, final_lines, q_gain, k_gain, out_ref,
+    in_gain, post_gain, final_gain, cos_ref, sin_ref,
     out_a, out_b, in_a, in_b, held_a, held_b, cols, proj, kv, query, mixed, wout,
     half_out, half_in, part_out, part_in, summed,
     xa_s, xa_r, xb_s, xb_r,
@@ -378,6 +422,9 @@
         return carry
 
     lax.fori_loop(1, 16, start_a, 0)
+    for gain, lines in ((in_gain, in_lines), (post_gain, post_lines), (final_gain, final_lines)):
+        for i in range(lines.shape[0]):
+            gain[:, i * 128:(i + 1) * 128] = lines[i:i + 1]
     in_a[tp] = out_a[tp]
     in_b[tp] = out_b[tp]
 
@@ -394,6 +441,16 @@
 
     lax.fori_loop(0, tokens // step_rows, norm_rows, 0)
     proj[...] = jnp.zeros_like(proj)
+    row_ids = ctx * tokens + lax.broadcasted_iota(jnp.int32, (tokens, 1), 0)
+    seg_start = jnp.zeros_like(row_ids)
+    begin = jnp.int32(0)
+    for i in range(lengths.shape[0]):
+        seg_start = jnp.maximum(seg_start, jnp.where(begin <= row_ids, begin, 0))
+        begin = begin + lengths[i]
+    angle = (row_ids - seg_start).astype(jnp.float32) * frequency[...]
+    low = lax.broadcasted_iota(jnp.int32, angle.shape, 1) < head // 2
+    cos_ref[...] = jnp.cos(angle)
+    sin_ref[...] = jnp.where(low, -jnp.sin(angle), jnp.sin(angle))
 
     class Gather:
         def __init__(self, held, got, ys, yr, zs, zr, fs, fr):
@@ -556,7 +613,7 @@
     value_rows = kv[:, :, head:].reshape(span, head)
     q_ids = ctx * tokens + lax.broadcasted_iota(jnp.int32, (tokens, span), 0)
     k_ids = (ctx - reach) * tokens + lax.broadcasted_iota(jnp.int32, (tokens, span), 1)
-    visible = (k_ids <= q_ids) & (q_ids - k_ids < WINDOW) & (k_ids >= start_ref[...])
+    visible = (k_ids <= q_ids) & (q_ids - k_ids < WINDOW) & (k_ids >= seg_start)
     for h in range(2):
         scores = lax.dot_general(
             query[h], key_rows, (((1,), (1,)), ((), ())), preferred_element_type=jnp.float32
@@ -651,7 +708,7 @@
 
 
 def layer(
-    send_slot, keep_from, row_of, slot_of, residual, stored, cosine, sine, seg_start,
+    send_slot, keep_from, row_of, slot_of, lengths, residual, stored, frequency,
     in_gain, q_gain, k_gain, post_gain, final_gain,
 ):
     tokens, depth = residual.shape
@@ -671,9 +728,11 @@
     return pl.pallas_call(
         layer_kernel,
         out_shape=jax.ShapeDtypeStruct((share, depth), bf16),
-        in_specs=[smem] * 4 + [vmem] * 10,
+        in_specs=[smem] * 5 + [vmem] * 8,
         out_specs=vmem,
-        scratch_shapes=[
+        scratch_shapes=[VMEM((1, depth), jnp.float32)] * 3
+        + [VMEM((tokens, head), jnp.float32)] * 2
+        + [
             VMEM((16, blk_rows, A_COLS), bf16),
             VMEM((16, blk_rows, b_cols), bf16),
             VMEM((16, blk_rows, A_COLS), bf16),
@@ -702,26 +761,22 @@
         ),
         name="layer",
     )(
-        send_slot, keep_from, row_of, slot_of, residual, stored, cosine, sine, seg_start[:, None],
-        in_gain[None], q_gain[None], k_gain[None], post_gain[None], final_gain[None],
+        send_slot, keep_from, row_of, slot_of, lengths, residual, stored, frequency,
+        in_gain.reshape(-1, 128), post_gain.reshape(-1, 128), final_gain.reshape(-1, 128),
+        q_gain[None], k_gain[None],
     )
 
 
-def rope_tables(position, head):
+def rope_frequency(head):
     half_size = head // 2
     frequency = rope_base ** (-2.0 * jnp.arange(half_size, dtype=jnp.float32) / head)
-    angle_rows = position.astype(jnp.float32)[:, None] * frequency[None, :]
-    cosine, sine = jnp.cos(angle_rows), jnp.sin(angle_rows)
-    return (
-        jnp.concatenate([cosine, cosine], axis=-1),
-        jnp.concatenate([-sine, sine], axis=-1),
-    )
+    return jnp.concatenate([frequency, frequency])[None]
 
 
 def block_tables(block_list, ctx_index, tp_index, ctx_count, tp_count, blocks_dev):
     rows_per_reader = blocks_dev * ctx_count
     grid = block_list.reshape(ctx_count, tp_count, blocks_dev)
-    readers = grid // rows_per_reader
+    readers = (grid * 1171) >> 16
     my_readers = lax.dynamic_slice(
         readers, (ctx_index, tp_index, 0), (1, 1, blocks_dev)
     ).reshape(-1)
@@ -730,7 +785,7 @@
     send_slot = jnp.sum(jnp.where(my_readers[None, :] == sources[:, None], slots[None, :], 0), axis=1)
     hit = readers == tp_index
     present = jnp.any(hit, axis=2)
-    row_index = jnp.sum(jnp.where(hit, grid % rows_per_reader, 0), axis=2)
+    row_index = jnp.sum(jnp.where(hit, grid - readers * rows_per_reader, 0), axis=2)
     before = sources[None, :] < sources[:, None]
     rank = jnp.sum((present[:, None, :] & before[None]).astype(jnp.int32), axis=2)
     chosen = (rank[:, None, :] == slots[None, :, None]) & present[:, None, :]
@@ -768,18 +823,12 @@
     tables = block_tables(
         block_list, ctx_index, tp_index, ctx_count, tp_count, stored_blocks.shape[0]
     )
-    seq_starts = jnp.cumsum(lengths) - lengths
-    query_ids = ctx_index * row_count + jnp.arange(row_count, dtype=jnp.int32)
-    seg_start = jnp.max(
-        jnp.where(seq_starts[None, :] <= query_ids[:, None], seq_starts[None, :], 0), axis=1
-    )
-    cosine, sine = rope_tables(query_ids - seg_start, HEAD_DIM)
     final = layer(
-        *tables, residual, stored_blocks, cosine, sine, seg_start,
+        *tables, lengths, residual, stored_blocks, rope_frequency(HEAD_DIM),
         in_gain, q_gain, k_gain, post_gain, final_gain,
     )
     all_rows = vocab_stats(final, vocab_table, actions)
-    ref_logprob = lax.dynamic_slice_in_dim(all_rows[0], tp_index * share_rows, share_rows, 0)
+    ref_logprob = lax.dynamic_slice_in_dim(all_rows.reshape(-1), tp_index * share_rows, share_rows, 0)
     return (ref_logprob, old_logprob - ref_logprob)
 
 

time: 241 us -> 222 us (0.921)
  Pallas kernels: 223 us -> 215 us
  local copies, waits for them, and re-layouts: 9.71 us -> 1.84 us
  other arithmetic: 7.27 us -> 4.22 us
    pallas_call x1, Pallas kernels: 92 us -> 83.7 us  [vocab_stats(): pl.pallas_call(vocab_kernel, out_shape=jax.ShapeDtypeStruct((2, 128), jnp...]
    broadcast_in_dim x3 -> x0, local copies, waits for them, and re-layouts: 4.06 us -> none  [the longest x1 1.36 us: layer(): in_gain[None]]
where the time goes in v3:
time: 222 us; the launch traced here: 221 us
  Pallas kernels  215 us (97%)
  other arithmetic  4.22 us (2%)
    pallas_call x1, Pallas kernels, layer(): pl.pallas_call(layer_kernel, out_shape=jax.ShapeDtypeStruct((share, depth...  131 us
    pallas_call x1, Pallas kernels, vocab_stats(): pl.pallas_call(vocab_kernel, out_shape=jax.ShapeDtypeStruct((2, 128), jnp...  83.7 us

profile of v3, /device:TPU:1, one launch (start us, length us, event | category | flops | bytes accessed | tf_op | source)
XLA Modules:
  0.0 221.4 jit_solution(6031373931164762355)
XLA Ops:
  0.6 0.0 copy-start.1
  0.7 0.6 maximum_bitcast_fusion.frequency
  1.3 0.1 iota_add_fusion
  1.4 0.1 add.95
  1.5 0.9 reshape.101
  2.4 0.2 fusion
  2.6 0.2 convert_reduce_fusion
  2.8 0.2 select_reduce_fusion
  3.0 0.3 select_reduce_fusion.2
  3.3 0.1 copy.15
  3.4 0.1 reshape.102.row_of
  3.5 0.0 copy-start
  3.5 0.7 select_reduce_fusion.1.slot_of
  4.2 0.7 dynamic-slice_reduce_fusion.keep_from
  4.9 0.6 select_reduce_fusion.4.send_slot
  5.5 0.0 copy-done
  5.5 130.9 %layer.1.fin_ref = bf16[16,5376]{1,0:T(8,128)(2,1)} custom-call(s32[16]{0:T(128)} %select_reduce_fusion.4.send_slot, s32[7]{0:T(128)} %dynamic-slice_reduce_fusion.keep_from, s32[56]{0:T(128)} %copy-done, s32[56]{0:T(128)} %select_reduce_fusion.1.slot_of, s32[4]{0:T(128)} %lengths.1, bf16[256,5376]{1,0:T(8,128)(2,1)} %residual_ref.1, ...), custom_call_target="tpu_custom_call" | custom-call | tf_op jit(solution)/shard_map/layer/pallas_call | solution.py:728
  136.4 83.7 %vocab_stats.1 = f32[2,128]{1,0:T(2,128)} custom-call(bf16[16,5376]{1,0:T(8,128)(2,1)} %layer.1.fin_ref, bf16[1152,5376]{1,0:T(8,128)(2,1)} %table_ref.1, s32[16,128]{1,0:T(8,128)} %bitcast.14), custom_call_target="tpu_custom_call" | custom-call | tf_op jit(solution)/shard_map/vocab_stats/pallas_call | solution.py:338
  220.1 0.0 copy-done.1
  220.1 1.2 fusion.8
  (4 shorter events, 0.0 us)
Async XLA Ops:
  0.6 219.5 %copy-start.1 = (f32[16]{0:T(128)S(1)}, f32[16]{0:T(128)}, u32[]{:S(2)}) copy-start(f32[16]{0:T(128)} %param.23) | copy-start | bytes 196
  3.5 2.0 copy-start

commit v4 on v3

--- a/solution.py
+++ b/solution.py
@@ -46,10 +46,12 @@
     return device_of(x, y, z, k + 1)
 
 
-def greet(peers):
+def greet(peers, meanwhile=None):
     barrier = pltpu.get_barrier_semaphore()
     for peer in peers:
         pl.semaphore_signal(barrier, inc=1, device_id=peer, device_id_type=MESH)
+    if meanwhile is not None:
+        meanwhile()
     pl.semaphore_wait(barrier, len(peers))
 
 
@@ -371,18 +373,17 @@
     )(fin, table, actions.reshape(-1, 128))
 
 
-A_COLS = 512
+CHUNK_AT = (1, 0, 2)
+Z_FIRST = (0, 0, 0)
 
 
 def layer_kernel(
     send_slot, keep_from, row_of, slot_of,
-    lengths, residual_ref, stored_ref, frequency, in_lines, post_lines, final_lines, q_gain, k_gain, out_ref,
+    lengths, residual_hbm, stored_hbm, frequency, in_lines, post_lines, final_lines, q_gain, k_gain, out_ref,
     in_gain, post_gain, final_gain, cos_ref, sin_ref,
-    out_a, out_b, in_a, in_b, held_a, held_b, cols, proj, kv, query, mixed, wout,
+    residual_ref, stored_ref, out, got_0, got_1, got_2, held, cols, proj, kv, query, mixed, wout,
     half_out, half_in, part_out, part_in, summed,
-    xa_s, xa_r, xb_s, xb_r,
-    ya_s, ya_r, za_s, za_r, fa_s, fa_r,
-    yb_s, yb_r, zb_s, zb_r, fb_s, fb_r,
+    load_sem, x_s, x_r, y_s, y_r, z_s, z_r, f_s, f_r,
     h_s, h_r, c_s, c_r, p_s, p_r,
 ):
     ctx = lax.axis_index("ctx")
@@ -405,28 +406,44 @@
     z_peer = lambda step: (y_hi * 4 + (z + step) % 4, tp)
     y_peer = ((ctx + 4) % 8, tp)
 
-    def swap(out, got, ss, rs, off):
-        return send(out.at[(tp + off) % 16], got.at[tp], ss.at[off], rs.at[off], t_peer(off))
+    got = (got_0, got_1, got_2)
+
+    def swap(i, off):
+        return send(
+            out.at[i, (tp + off) % 16], got[i].at[tp], x_s.at[i, off], x_r.at[i, off], t_peer(off)
+        )
+
+    stored_copy = pltpu.make_async_copy(stored_hbm, stored_ref, load_sem.at[0])
+    residual_copy = pltpu.make_async_copy(residual_hbm, residual_ref, load_sem.at[1])
+    stored_copy.start()
+    residual_copy.start()
+    chunk = out.shape[3]
 
     def stage(t, carry):
         block = stored_ref[send_slot[t]]
-        out_a[t] = block[:, :A_COLS]
-        out_b[t] = block[:, A_COLS:]
-        return carry
-
-    lax.fori_loop(0, 16, stage, 0)
-    greet([((ctx + o) % 8, tp) for o in range(1, 8)] + [t_peer(o) for o in range(1, 16)])
-
-    def start_a(off, carry):
-        swap(out_a, in_a, xa_s, xa_r, off).start()
-        return carry
-
-    lax.fori_loop(1, 16, start_a, 0)
+        for i, at in enumerate(CHUNK_AT):
+            out[i, t] = block[:, at * chunk:(at + 1) * chunk]
+        return carry
+
+    def stage_all():
+        stored_copy.wait()
+        lax.fori_loop(0, 16, stage, 0)
+
+    greet(
+        [((ctx + o) % 8, tp) for o in range(1, 8)] + [t_peer(o) for o in range(1, 16)], stage_all
+    )
+
+    def start_swap(off, carry):
+        swap(0, off).start()
+        return carry
+
+    lax.fori_loop(1, 16, start_swap, 0)
+    residual_copy.wait()
     for gain, lines in ((in_gain, in_lines), (post_gain, post_lines), (final_gain, final_lines)):
         for i in range(lines.shape[0]):
             gain[:, i * 128:(i + 1) * 128] = lines[i:i + 1]
-    in_a[tp] = out_a[tp]
-    in_b[tp] = out_b[tp]
+    for i in range(3):
+        got[i][tp] = out[i, tp]
 
     step_rows = 32
 
@@ -452,127 +469,141 @@
     cos_ref[...] = jnp.cos(angle)
     sin_ref[...] = jnp.where(low, -jnp.sin(angle), jnp.sin(angle))
 
-    class Gather:
-        def __init__(self, held, got, ys, yr, zs, zr, fs, fr):
-            self.held, self.got = held, got
-            self.ys, self.yr, self.zs, self.zr, self.fs, self.fr = ys, yr, zs, zr, fs, fr
-
-        def y(self, k):
-            return send(self.held.at[0, 0, k], self.held.at[1, 0, k], self.ys.at[k], self.yr.at[k], y_peer)
-
-        def z(self, yy, step, k):
-            i = 0 if step == 1 else 1
-            return send(
-                self.held.at[yy, 0, k], self.held.at[yy, (4 - step) % 4, k],
-                self.zs.at[yy, i, k], self.zr.at[yy, i, k], z_peer(step),
-            )
-
-        def f(self, yy, step, k):
-            return send(
-                self.held.at[yy, 3 if step == 1 else 1, k], self.held.at[yy, 2, k],
-                self.fs.at[yy, k], self.fr.at[yy, k], z_peer(step),
-            )
-
-        def own(self, k):
-            self.held[0, 0, k] = self.got[keep_from[k]]
-            self.y(k).start()
-            self.z(0, 1, k).start()
-            self.z(0, 3, k).start()
-
-        def partner(self, k):
-            self.y(k).wait_recv()
-            self.z(1, 1, k).start()
-            self.z(1, 3, k).start()
-
-        def side(self, yy, k):
-            right = k < 4 - yy
-            self.z(yy, 1, k).wait_recv()
-
-            @pl.when(right)
-            def _():
-                self.f(yy, 1, k).start()
-
-            self.z(yy, 3, k).wait_recv()
-
-            @pl.when(jnp.logical_not(right))
-            def _():
-                self.f(yy, 3, k).start()
-
-        def far(self, yy, k):
-            self.f(yy, 1, k).wait_recv()
-
-        def sent(self, k):
-            self.y(k).wait_send()
-            for yy in range(2):
-                self.z(yy, 1, k).wait_send()
-                self.z(yy, 3, k).wait_send()
-                self.f(yy, 1, k).wait_send()
-
-    ga = Gather(held_a, in_a, ya_s, ya_r, za_s, za_r, fa_s, fa_r)
-    gb = Gather(held_b, in_b, yb_s, yb_r, zb_s, zb_r, fb_s, fb_r)
-
-    def term(yy, zz, k):
-        c = (y_hi + yy) % 2 * 4 + (z + zz) % 4
-        r = row_of[c * n_blk + k]
-        proj[...] += jnp.dot(
-            cols[r, :, :blk_rows], held_a[yy, zz, k], preferred_element_type=jnp.float32
-        )
-
-    def each_block(body):
+    def early(i):
+        return n_blk - Z_FIRST[i]
+
+    def y_copy(i, zz, k):
+        return send(
+            held.at[i, 0, zz, k], held.at[i, 1, zz, k], y_s.at[i, zz, k], y_r.at[i, zz, k], y_peer
+        )
+
+    def z_copy(i, yy, step, k):
+        j = 0 if step == 1 else 1
+        return send(
+            held.at[i, yy, 0, k], held.at[i, yy, 4 - step, k],
+            z_s.at[i, yy, j, k], z_r.at[i, yy, j, k], z_peer(step),
+        )
+
+    def f_copy(i, yy, step, k):
+        return send(
+            held.at[i, yy, 3 if step == 1 else 1, k], held.at[i, yy, 2, k],
+            f_s.at[i, yy, k], f_r.at[i, yy, k], z_peer(step),
+        )
+
+    def blocks(body, low=0, high=None):
         def run(k, carry):
             body(k)
             return carry
 
-        lax.fori_loop(0, n_blk, run, 0)
-
-    def wait_a(off, carry):
-        swap(out_a, in_a, xa_s, xa_r, off).wait_recv()
-        return carry
-
-    lax.fori_loop(1, 16, wait_a, 0)
-    each_block(ga.own)
-
-    def start_b(off, carry):
-        swap(out_b, in_b, xb_s, xb_r, off).start()
-        return carry
-
-    lax.fori_loop(1, 16, start_b, 0)
-
-    def one(k):
-        ga.partner(k)
-        term(0, 0, k)
-
-    def two(k):
-        ga.side(0, k)
-        term(0, 3, k)
-        term(0, 1, k)
-
-    def three(k):
-        ga.side(1, k)
-        term(1, 0, k)
-        term(1, 3, k)
-        term(1, 1, k)
-
-    def four(yy):
-        def run(k):
-            ga.far(yy, k)
-            term(yy, 2, k)
-
-        return run
-
-    each_block(one)
-    each_block(two)
-    each_block(three)
-
-    def wait_b(off, carry):
-        swap(out_b, in_b, xb_s, xb_r, off).wait_recv()
-        return carry
-
-    lax.fori_loop(1, 16, wait_b, 0)
-    each_block(gb.own)
-    each_block(four(0))
-    each_block(gb.partner)
-    each_block(four(1))
+        lax.fori_loop(low, n_blk if high is None else high, run, 0)
+
+    def own(i):
+        def wait(off, carry):
+            swap(i, off).wait_recv()
+            return carry
+
+        def body(k):
+            held[i, 0, 0, k] = got[i][keep_from[k]]
+            y_copy(i, 0, k).start()
+            z_copy(i, 0, 1, k).start()
+            z_copy(i, 0, 3, k).start()
+            if i < 2:
+                swap(i + 1, 2 * k + 1).start()
+                swap(i + 1, 2 * k + 2).start()
+
+        lax.fori_loop(1, 16, wait, 0)
+        blocks(body)
+        if i < 2:
+            swap(i + 1, 15).start()
+
+    def partner(i):
+        def body(k):
+            y_copy(i, 0, k).wait_recv()
+
+            @pl.when(k < early(i))
+            def _():
+                z_copy(i, 1, 1, k).start()
+                z_copy(i, 1, 3, k).start()
+
+            term(i, 0, 0, k)
+            term(i, 1, 0, k)
+
+        blocks(body)
+
+    def side(i, yy):
+        turn = 4 if yy == 0 else early(i) // 2
+
+        def body(k):
+            z_copy(i, yy, 1, k).wait_recv()
+
+            @pl.when(k < turn)
+            def _():
+                f_copy(i, yy, 1, k).start()
+
+            z_copy(i, yy, 3, k).wait_recv()
+
+            @pl.when(k >= turn)
+            def _():
+                f_copy(i, yy, 3, k).start()
+
+            if yy == 0:
+                @pl.when(k >= early(i))
+                def _():
+                    y_copy(i, 3, k).start()
+                    y_copy(i, 1, k).start()
+
+            term(i, yy, 3, k)
+            term(i, yy, 1, k)
+
+        def across(k):
+            y_copy(i, 3, k).wait_recv()
+            y_copy(i, 1, k).wait_recv()
+            term(i, 1, 3, k)
+            term(i, 1, 1, k)
+
+        if yy == 0:
+            blocks(body)
+        else:
+            blocks(body, 0, early(i))
+            blocks(across, early(i))
+
+    def far(i, yy):
+        def body(k):
+            f_copy(i, yy, 1, k).wait_recv()
+            if yy == 0:
+                @pl.when(k >= early(i))
+                def _():
+                    y_copy(i, 2, k).start()
+            term(i, yy, 2, k)
+
+        def across(k):
+            y_copy(i, 2, k).wait_recv()
+            term(i, 1, 2, k)
+
+        if yy == 0:
+            blocks(body)
+        else:
+            blocks(body, 0, early(i))
+            blocks(across, early(i))
+
+    def term(i, yy, zz, k):
+        if CHUNK_AT[i] < 2:
+            c = (y_hi + yy) % 2 * 4 + (z + zz) % 4
+            at = CHUNK_AT[i] * chunk
+            proj[:, at:at + chunk] += jnp.dot(
+                cols[row_of[c * n_blk + k], :, :blk_rows], held[i, yy, zz, k],
+                preferred_element_type=jnp.float32,
+            )
+
+    own(0)
+    partner(0)
+    own(1)
+    side(0, 0)
+    partner(1)
+    side(0, 1)
+    far(0, 0)
+    side(1, 0)
+    far(0, 1)
 
     def heads(at, gain):
         e = proj[:, pl.ds(at * head, head)]
@@ -599,10 +630,15 @@
         def _():
             kv[reach - step] = jnp.zeros(kv.shape[1:], kv.dtype)
 
+    side(1, 1)
+    own(2)
+    far(1, 0)
+    partner(2)
+    far(1, 1)
     for h in range(2):
         query[h] = heads(h, q_gain)
-    for yy in range(2):
-        each_block(lambda k: gb.side(yy, k))
+    side(2, 0)
+    side(2, 1)
     for step in range(1, reach + 1):
         @pl.when(ctx >= step)
         def _():
@@ -620,14 +656,14 @@
         ) * QUERY_SCALAR ** (-0.5)
         probs = jnp.where(visible, jnp.exp(scores), 0.0)
         probs = (probs / jnp.sum(probs, axis=1, keepdims=True)).astype(jnp.bfloat16)
-        got = jnp.dot(probs, value_rows, preferred_element_type=jnp.float32).astype(jnp.bfloat16)
-        mixed[:, :, :, h * head:(h + 1) * head] = got.reshape(8, 2, tokens // 16, head)
-
-    for yy in range(2):
-        each_block(lambda k: gb.far(yy, k))
+        heard = jnp.dot(probs, value_rows, preferred_element_type=jnp.float32).astype(jnp.bfloat16)
+        mixed[:, :, :, h * head:(h + 1) * head] = heard.reshape(8, 2, tokens // 16, head)
+
+    far(2, 0)
+    far(2, 1)
 
     def order(r, carry):
-        wout[r] = held_b.reshape(8 * n_blk, blk_rows, 2 * head)[slot_of[r]]
+        wout[r] = held.at[2].reshape(8 * n_blk, blk_rows, chunk)[slot_of[r]]
         return carry
 
     lax.fori_loop(0, depth // blk_rows, order, 0)
@@ -686,13 +722,30 @@
     out_ref[...] = rms(hidden, final_gain).astype(jnp.bfloat16)
 
     def swapped(off, carry):
-        swap(out_a, in_a, xa_s, xa_r, off).wait_send()
-        swap(out_b, in_b, xb_s, xb_r, off).wait_send()
+        for i in range(3):
+            swap(i, off).wait_send()
         return carry
 
     lax.fori_loop(1, 16, swapped, 0)
-    each_block(ga.sent)
-    each_block(gb.sent)
+    for i in range(3):
+        def sent(k):
+            y_copy(i, 0, k).wait_send()
+            z_copy(i, 0, 1, k).wait_send()
+            z_copy(i, 0, 3, k).wait_send()
+            f_copy(i, 0, 1, k).wait_send()
+
+        def sent_z(k):
+            z_copy(i, 1, 1, k).wait_send()
+            z_copy(i, 1, 3, k).wait_send()
+            f_copy(i, 1, 1, k).wait_send()
+
+        def sent_y(k):
+            for zz in range(1, 4):
+                y_copy(i, zz, k).wait_send()
+
+        blocks(sent)
+        blocks(sent_z, 0, early(i))
+        blocks(sent_y, early(i))
     for step in range(1, reach + 1):
         @pl.when(ctx + step < 8)
         def _():
@@ -721,38 +774,41 @@
     piece = depth // n_pieces
     reach = WINDOW // tokens
     dma = pltpu.SemaphoreType.DMA
-    b_cols = width - A_COLS
+    chunk = width // 3
     smem = pl.BlockSpec(memory_space=pltpu.SMEM)
     vmem = pl.BlockSpec(memory_space=VMEM)
-    gather_sems = [dma((n_blk,))] * 2 + [dma((2, 2, n_blk))] * 2 + [dma((2, n_blk))] * 2
     return pl.pallas_call(
         layer_kernel,
         out_shape=jax.ShapeDtypeStruct((share, depth), bf16),
-        in_specs=[smem] * 5 + [vmem] * 8,
+        in_specs=[smem] * 5 + [pl.BlockSpec(memory_space=pl.ANY)] * 2 + [vmem] * 6,
         out_specs=vmem,
         scratch_shapes=[VMEM((1, depth), jnp.float32)] * 3
         + [VMEM((tokens, head), jnp.float32)] * 2
         + [
-            VMEM((16, blk_rows, A_COLS), bf16),
-            VMEM((16, blk_rows, b_cols), bf16),
-            VMEM((16, blk_rows, A_COLS), bf16),
-            VMEM((16, blk_rows, b_cols), bf16),
-            VMEM((2, 4, n_blk, blk_rows, A_COLS), bf16),
-            VMEM((2, 4, n_blk, blk_rows, b_cols), bf16),
+            VMEM((tokens, depth), bf16),
+            VMEM((n_blk, blk_rows, width), bf16),
+            VMEM((3, 16, blk_rows, chunk), bf16),
+            VMEM((16, blk_rows, chunk), bf16),
+            VMEM((16, blk_rows, chunk), bf16),
+            VMEM((16, blk_rows, chunk), bf16),
+            VMEM((3, 2, 4, n_blk, blk_rows, chunk), bf16),
             VMEM((n_rows, tokens, 128), bf16),
-            VMEM((tokens, A_COLS), jnp.float32),
+            VMEM((tokens, 2 * chunk), jnp.float32),
             VMEM((reach + 1, tokens, 2 * head), bf16),
             VMEM((2, tokens, head), bf16),
             VMEM((8, 2, share, 2 * head), bf16),
-            VMEM((n_rows, blk_rows, b_cols), bf16),
+            VMEM((n_rows, blk_rows, chunk), bf16),
             VMEM((n_pieces, 8, share, piece), bf16),
             VMEM((n_pieces, 8, share, piece), bf16),
             VMEM((n_pieces, 8, share, piece), bf16),
             VMEM((n_pieces, 8, share, piece), bf16),
             VMEM((share, depth), jnp.float32),
         ]
-        + [dma((16,))] * 4
-        + gather_sems * 2
+        + [dma((2,))]
+        + [dma((3, 16))] * 2
+        + [dma((3, 4, n_blk))] * 2
+        + [dma((3, 2, 2, n_blk))] * 2
+        + [dma((3, 2, n_blk))] * 2
         + [dma((reach,))] * 2
         + [dma((n_pieces,))] * 2
         + [dma((n_pieces, 8))] * 2,

time: 222 us -> 213 us (0.959)
  Pallas kernels: 215 us -> 206 us
    pallas_call x1, Pallas kernels: 131 us -> 121 us  [layer(): pl.pallas_call(layer_kernel, out_shape=jax.ShapeDtypeStruct((share, depth...]
where the time goes in v4:
time: 213 us
  Pallas kernels  206 us (97%)
  other arithmetic  4.22 us (2%)
    pallas_call x1, Pallas kernels, layer(): pl.pallas_call(layer_kernel, out_shape=jax.ShapeDtypeStruct((share, depth...  121 us
    pallas_call x1, Pallas kernels, vocab_stats(): pl.pallas_call(vocab_kernel, out_shape=jax.ShapeDtypeStruct((2, 128), jnp...  85.5 us

profile of v4, /device:TPU:1, one launch (start us, length us, event | category | flops | bytes accessed | tf_op | source)
XLA Modules:
  0.0 213.2 jit_solution(10086164752101166838)
XLA Ops:
  0.6 0.0 copy-start.1
  0.7 0.6 maximum_bitcast_fusion.frequency
  1.3 0.1 iota_add_fusion
  1.4 0.1 add.95
  1.5 0.9 reshape.101
  2.4 0.2 fusion
  2.6 0.2 convert_reduce_fusion
  2.8 0.2 select_reduce_fusion
  3.0 0.3 select_reduce_fusion.2
  3.3 0.1 copy.15
  3.4 0.1 reshape.102.row_of
  3.5 0.0 copy-start
  3.5 0.7 select_reduce_fusion.1.slot_of
  4.2 0.7 dynamic-slice_reduce_fusion.keep_from
  4.9 0.6 select_reduce_fusion.4.send_slot
  5.5 0.0 copy-done
  5.5 120.9 %layer.1.fin_ref = bf16[16,5376]{1,0:T(8,128)(2,1)} custom-call(s32[16]{0:T(128)} %select_reduce_fusion.4.send_slot, s32[7]{0:T(128)} %dynamic-slice_reduce_fusion.keep_from, s32[56]{0:T(128)} %copy-done, s32[56]{0:T(128)} %select_reduce_fusion.1.slot_of, s32[4]{0:T(128)} %lengths.1, bf16[256,5376]{1,0:T(8,128)(2,1)} %residual_hbm.1, ...), custom_call_target="tpu_custom_call" | custom-call | tf_op jit(solution)/shard_map/layer/pallas_call | solution.py:780
  126.4 85.5 %vocab_stats.1 = f32[2,128]{1,0:T(2,128)} custom-call(bf16[16,5376]{1,0:T(8,128)(2,1)} %layer.1.fin_ref, bf16[1152,5376]{1,0:T(8,128)(2,1)} %table_ref.1, s32[16,128]{1,0:T(8,128)} %bitcast.14), custom_call_target="tpu_custom_call" | custom-call | tf_op jit(solution)/shard_map/vocab_stats/pallas_call | solution.py:340
  211.9 0.0 copy-done.1
  211.9 1.2 fusion.8
  (4 shorter events, 0.0 us)
Async XLA Ops:
  0.6 211.3 %copy-start.1 = (f32[16]{0:T(128)S(1)}, f32[16]{0:T(128)}, u32[]{:S(2)}) copy-start(f32[16]{0:T(128)} %param.23) | copy-start | bytes 196
  3.5 2.0 copy-start

commit v5 on v4

--- a/solution.py
+++ b/solution.py
@@ -1,5 +1,8 @@
+import functools
+
 import jax
 import jax.numpy as jnp
+import numpy as np
 from jax import lax
 from jax.experimental import pallas as pl
 from jax.experimental.pallas import tpu as pltpu
@@ -55,10 +58,10 @@
     pl.semaphore_wait(barrier, len(peers))
 
 
-def vocab_kernel(
-    fin_ref, table_ref, actions_ref, out_ref,
-    buf, table, acc, part_exp, part_hit, column, st1, r1, st2, r2,
+def vocab_part(
+    fin_ref, table_ref, actions_ref, out_ref, buf, r1, r2,
     table_sem, s1, v1, s2, v2, s3, v3, sf, vf, sk, vk, sa, va, sb, vb,
+    table, acc, part_exp, part_hit, column, st1, st2,
 ):
     ctx = lax.axis_index("ctx")
     tp = lax.axis_index("tp")
@@ -77,11 +80,8 @@
         table_copy(p).start()
     for p in range(3):
         buf[p, 0, 0, core, 0] = fin_ref[:, pl.ds(p * width, width)]
-    x, y, z, k = coords()
     c_peer = lambda off: ((ctx + off) % 8, tp)
     t_peer = lambda off: (ctx, (tp + off) % 16)
-    far_y = device_of(x, y - 1 + 2 * (y % 2), z, k)
-    greet([c_peer(o) for o in range(1, 8)] + [t_peer(o) for o in range(1, 16)] + [far_y])
 
     def send(src, dst, send_sem, recv_sem, peer):
         return pltpu.make_async_remote_copy(
@@ -332,59 +332,17 @@
         stage2(off).wait_send()
 
 
-def vocab_stats(fin, table, actions):
-    rows, depth = fin.shape
-    width = depth // 3
-    vocab_rows = table.shape[0]
-    dma = pltpu.SemaphoreType.DMA
-    return pl.pallas_call(
-        vocab_kernel,
-        out_shape=jax.ShapeDtypeStruct((2, 128), jnp.float32),
-        in_specs=[
-            pl.BlockSpec(memory_space=VMEM),
-            pl.BlockSpec(memory_space=pl.ANY),
-            pl.BlockSpec(memory_space=VMEM),
-        ],
-        out_specs=pl.BlockSpec(memory_space=VMEM),
-        scratch_shapes=[
-            VMEM((3, 4, 4, 2, 4, rows, width), jnp.bfloat16),
-            VMEM((3, vocab_rows, width), jnp.bfloat16),
-            VMEM((128, rows, vocab_rows), jnp.float32),
-            VMEM((128, rows, 128), jnp.float32),
-            VMEM((128, rows, 128), jnp.float32),
-            VMEM((128, rows, 1), jnp.int32),
-            VMEM((8, 8, 128), jnp.float32),
-            VMEM((8, 8, 128), jnp.float32),
-            VMEM((8, 128), jnp.float32),
-            VMEM((16, 8, 128), jnp.float32),
-            dma((3,)),
-            dma((3, 3)), dma((3, 3)),
-            dma((3, 4)), dma((3, 4)),
-            dma((3, 4, 4)), dma((3, 4, 4)),
-            dma((3, 4)), dma((3, 4)),
-            dma((3, 4, 4)), dma((3, 4, 4)),
-            dma((8,)), dma((8,)),
-            dma((16,)), dma((16,)),
-        ],
-        compiler_params=pltpu.CompilerParams(
-            collective_id=2, has_side_effects=True, vmem_limit_bytes=60 * 2**20
-        ),
-        name="vocab_stats",
-    )(fin, table, actions.reshape(-1, 128))
-
-
 CHUNK_AT = (1, 0, 2)
-Z_FIRST = (0, 0, 0)
-
-
-def layer_kernel(
+Z_FIRST = (0, 0, 2)
+
+
+def layer_part(
     send_slot, keep_from, row_of, slot_of,
     lengths, residual_hbm, stored_hbm, frequency, in_lines, post_lines, final_lines, q_gain, k_gain, out_ref,
-    in_gain, post_gain, final_gain, cos_ref, sin_ref,
-    residual_ref, stored_ref, out, got_0, got_1, got_2, held, cols, proj, kv, query, mixed, wout,
-    half_out, half_in, part_out, part_in, summed,
-    load_sem, x_s, x_r, y_s, y_r, z_s, z_r, f_s, f_r,
-    h_s, h_r, c_s, c_r, p_s, p_r,
+    got_0, got_1, got_2, held, kv, half_in, part_in,
+    load_sem, x_s, x_r, y_s, y_r, z_s, z_r, f_s, f_r, h_s, h_r, c_s, c_r, p_s, p_r,
+    in_gain, post_gain, final_gain, cos_ref, sin_ref, residual_ref, stored_ref, out, cols, proj,
+    query, mixed, wout, half_out, part_out, summed,
 ):
     ctx = lax.axis_index("ctx")
     tp = lax.axis_index("tp")
@@ -429,8 +387,11 @@
         stored_copy.wait()
         lax.fori_loop(0, 16, stage, 0)
 
+    x_at, y_at, z_at, k_at = coords()
+    far_y = device_of(x_at, y_at - 1 + 2 * (y_at % 2), z_at, k_at)
     greet(
-        [((ctx + o) % 8, tp) for o in range(1, 8)] + [t_peer(o) for o in range(1, 16)], stage_all
+        [((ctx + o) % 8, tp) for o in range(1, 8)] + [t_peer(o) for o in range(1, 16)] + [far_y],
+        stage_all,
     )
 
     def start_swap(off, carry):
@@ -707,20 +668,6 @@
 
     lax.fori_loop(0, n_pieces, give, 0)
     lax.fori_loop(0, n_pieces, take, 0)
-    for n in range(n_pieces):
-        total = part_out[n, chip].astype(jnp.float32)
-        for off in range(1, 8):
-            to_chip(n, off).wait_recv()
-            total = total + part_in[n, off].astype(jnp.float32)
-        summed[:, n * piece:(n + 1) * piece] = total
-
-    def rms(values, gain):
-        return values * lax.rsqrt(jnp.mean(values * values, axis=-1, keepdims=True) + epsilon) * gain[...]
-
-    mine = residual_ref[pl.ds(pl.multiple_of(tp * share, share), share)].astype(jnp.float32)
-    hidden = mine + rms(summed[...], post_gain)
-    out_ref[...] = rms(hidden, final_gain).astype(jnp.bfloat16)
-
     def swapped(off, carry):
         for i in range(3):
             swap(i, off).wait_send()
@@ -751,8 +698,26 @@
         def _():
             halo(step).wait_send()
 
+    def halves_sent(n, carry):
+        between(n).wait_send()
+        return carry
+
+    lax.fori_loop(0, n_pieces, halves_sent, 0)
+    for n in range(n_pieces):
+        total = part_out[n, chip].astype(jnp.float32)
+        for off in range(1, 8):
+            to_chip(n, off).wait_recv()
+            total = total + part_in[n, off].astype(jnp.float32)
+        summed[:, n * piece:(n + 1) * piece] = total
+
+    def rms(values, gain):
+        return values * lax.rsqrt(jnp.mean(values * values, axis=-1, keepdims=True) + epsilon) * gain[...]
+
+    mine = residual_ref[pl.ds(pl.multiple_of(tp * share, share), share)].astype(jnp.float32)
+    hidden = mine + rms(summed[...], post_gain)
+    out_ref[...] = rms(hidden, final_gain).astype(jnp.bfloat16)
+
     def parts_sent(n, carry):
-        between(n).wait_send()
         for off in range(1, 8):
             to_chip(n, off).wait_send()
         return carry
@@ -760,73 +725,123 @@
     lax.fori_loop(0, n_pieces, parts_sent, 0)
 
 
-def layer(
-    send_slot, keep_from, row_of, slot_of, lengths, residual, stored, frequency,
-    in_gain, q_gain, k_gain, post_gain, final_gain,
+def whole_kernel(counts, *refs):
+    n_tables, n_layer, n_layer_own, n_vocab_own = counts
+    tables, refs = refs[:n_tables], refs[n_tables:]
+    (lengths, residual, stored, frequency, in_lines, post_lines, final_lines, q_gain, k_gain,
+     table, actions, out_ref, fin), refs = refs[:13], refs[13:]
+    layer_refs, vocab_refs = refs[:n_layer], refs[n_layer:]
+    pl.run_scoped(
+        lambda *own: layer_part(
+            *tables, lengths, residual, stored, frequency, in_lines, post_lines, final_lines,
+            q_gain, k_gain, fin, *layer_refs, *own,
+        ),
+        *n_layer_own,
+    )
+    pl.run_scoped(
+        lambda *own: vocab_part(fin, table, actions, out_ref, *vocab_refs, *own), *n_vocab_own
+    )
+
+
+def whole(
+    tables, lengths, residual, stored, frequency, in_gain, q_gain, k_gain, post_gain, final_gain,
+    vocab_table, actions,
 ):
     tokens, depth = residual.shape
     n_blk, blk_rows, width = stored.shape
+    vocab_rows = vocab_table.shape[0]
     head = q_gain.shape[0]
     share = tokens // 16
-    bf16 = jnp.bfloat16
+    bf16, f32 = jnp.bfloat16, jnp.float32
     n_rows = depth // blk_rows
     n_pieces = 7
     piece = depth // n_pieces
     reach = WINDOW // tokens
+    chunk = width // 3
+    third = depth // 3
     dma = pltpu.SemaphoreType.DMA
-    chunk = width // 3
     smem = pl.BlockSpec(memory_space=pltpu.SMEM)
     vmem = pl.BlockSpec(memory_space=VMEM)
+    far = pl.BlockSpec(memory_space=pl.ANY)
+    layer_refs = [
+        VMEM((16, blk_rows, chunk), bf16),
+        VMEM((16, blk_rows, chunk), bf16),
+        VMEM((16, blk_rows, chunk), bf16),
+        VMEM((3, 2, 4, n_blk, blk_rows, chunk), bf16),
+        VMEM((reach + 1, tokens, 2 * head), bf16),
+        VMEM((n_pieces, 8, share, piece), bf16),
+        VMEM((n_pieces, 8, share, piece), bf16),
+        dma((2,)),
+        dma((3, 16)), dma((3, 16)),
+        dma((3, 4, n_blk)), dma((3, 4, n_blk)),
+        dma((3, 2, 2, n_blk)), dma((3, 2, 2, n_blk)),
+        dma((3, 2, n_blk)), dma((3, 2, n_blk)),
+        dma((reach,)), dma((reach,)),
+        dma((n_pieces,)), dma((n_pieces,)),
+        dma((n_pieces, 8)), dma((n_pieces, 8)),
+    ]
+    layer_own = [
+        VMEM((1, depth), f32),
+        VMEM((1, depth), f32),
+        VMEM((1, depth), f32),
+        VMEM((tokens, head), f32),
+        VMEM((tokens, head), f32),
+        VMEM((tokens, depth), bf16),
+        VMEM((n_blk, blk_rows, width), bf16),
+        VMEM((3, 16, blk_rows, chunk), bf16),
+        VMEM((n_rows, tokens, 128), bf16),
+        VMEM((tokens, 2 * chunk), f32),
+        VMEM((2, tokens, head), bf16),
+        VMEM((8, 2, share, 2 * head), bf16),
+        VMEM((n_rows, blk_rows, chunk), bf16),
+        VMEM((n_pieces, 8, share, piece), bf16),
+        VMEM((n_pieces, 8, share, piece), bf16),
+        VMEM((share, depth), f32),
+    ]
+    vocab_refs = [
+        VMEM((3, 4, 4, 2, 4, share, third), bf16),
+        VMEM((8, 8, 128), f32),
+        VMEM((16, 8, 128), f32),
+        dma((3,)),
+        dma((3, 3)), dma((3, 3)),
+        dma((3, 4)), dma((3, 4)),
+        dma((3, 4, 4)), dma((3, 4, 4)),
+        dma((3, 4)), dma((3, 4)),
+        dma((3, 4, 4)), dma((3, 4, 4)),
+        dma((8,)), dma((8,)),
+        dma((16,)), dma((16,)),
+    ]
+    vocab_own = [
+        VMEM((3, vocab_rows, third), bf16),
+        VMEM((128, share, vocab_rows), f32),
+        VMEM((128, share, 128), f32),
+        VMEM((128, share, 128), f32),
+        VMEM((128, share, 1), jnp.int32),
+        VMEM((8, 8, 128), f32),
+        VMEM((8, 128), f32),
+    ]
+    counts = (len(tables), len(layer_refs), layer_own, vocab_own)
     return pl.pallas_call(
-        layer_kernel,
-        out_shape=jax.ShapeDtypeStruct((share, depth), bf16),
-        in_specs=[smem] * 5 + [pl.BlockSpec(memory_space=pl.ANY)] * 2 + [vmem] * 6,
+        functools.partial(whole_kernel, counts),
+        out_shape=jax.ShapeDtypeStruct((2, 128), f32),
+        in_specs=[smem] * 5 + [far] * 2 + [vmem] * 6 + [far, vmem],
         out_specs=vmem,
-        scratch_shapes=[VMEM((1, depth), jnp.float32)] * 3
-        + [VMEM((tokens, head), jnp.float32)] * 2
-        + [
-            VMEM((tokens, depth), bf16),
-            VMEM((n_blk, blk_rows, width), bf16),
-            VMEM((3, 16, blk_rows, chunk), bf16),
-            VMEM((16, blk_rows, chunk), bf16),
-            VMEM((16, blk_rows, chunk), bf16),
-            VMEM((16, blk_rows, chunk), bf16),
-            VMEM((3, 2, 4, n_blk, blk_rows, chunk), bf16),
-            VMEM((n_rows, tokens, 128), bf16),
-            VMEM((tokens, 2 * chunk), jnp.float32),
-            VMEM((reach + 1, tokens, 2 * head), bf16),
-            VMEM((2, tokens, head), bf16),
-            VMEM((8, 2, share, 2 * head), bf16),
-            VMEM((n_rows, blk_rows, chunk), bf16),
-            VMEM((n_pieces, 8, share, piece), bf16),
-            VMEM((n_pieces, 8, share, piece), bf16),
-            VMEM((n_pieces, 8, share, piece), bf16),
-            VMEM((n_pieces, 8, share, piece), bf16),
-            VMEM((share, depth), jnp.float32),
-        ]
-        + [dma((2,))]
-        + [dma((3, 16))] * 2
-        + [dma((3, 4, n_blk))] * 2
-        + [dma((3, 2, 2, n_blk))] * 2
-        + [dma((3, 2, n_blk))] * 2
-        + [dma((reach,))] * 2
-        + [dma((n_pieces,))] * 2
-        + [dma((n_pieces, 8))] * 2,
+        scratch_shapes=[VMEM((share, depth), bf16)] + layer_refs + vocab_refs,
         compiler_params=pltpu.CompilerParams(
-            collective_id=1, has_side_effects=True, vmem_limit_bytes=60 * 2**20
+            collective_id=1, has_side_effects=True, vmem_limit_bytes=63 * 2**20
         ),
-        name="layer",
+        name="whole",
     )(
-        send_slot, keep_from, row_of, slot_of, lengths, residual, stored, frequency,
+        *tables, lengths, residual, stored, frequency,
         in_gain.reshape(-1, 128), post_gain.reshape(-1, 128), final_gain.reshape(-1, 128),
-        q_gain[None], k_gain[None],
+        q_gain[None], k_gain[None], vocab_table, actions.reshape(-1, 128),
     )
 
 
 def rope_frequency(head):
     half_size = head // 2
-    frequency = rope_base ** (-2.0 * jnp.arange(half_size, dtype=jnp.float32) / head)
-    return jnp.concatenate([frequency, frequency])[None]
+    frequency = rope_base ** (-2.0 * np.arange(half_size, dtype=np.float64) / head)
+    return jnp.asarray(np.concatenate([frequency, frequency])[None].astype(np.float32))
 
 
 def block_tables(block_list, ctx_index, tp_index, ctx_count, tp_count, blocks_dev):
@@ -879,11 +894,10 @@
     tables = block_tables(
         block_list, ctx_index, tp_index, ctx_count, tp_count, stored_blocks.shape[0]
     )
-    final = layer(
-        *tables, lengths, residual, stored_blocks, rope_frequency(HEAD_DIM),
-        in_gain, q_gain, k_gain, post_gain, final_gain,
+    all_rows = whole(
+        tables, lengths, residual, stored_blocks, rope_frequency(HEAD_DIM),
+        in_gain, q_gain, k_gain, post_gain, final_gain, vocab_table, actions,
     )
-    all_rows = vocab_stats(final, vocab_table, actions)
     ref_logprob = lax.dynamic_slice_in_dim(all_rows.reshape(-1), tp_index * share_rows, share_rows, 0)
     return (ref_logprob, old_logprob - ref_logprob)
 

time: 213 us -> 207 us (0.972)
  Pallas kernels: 206 us -> 201 us
    pallas_call x2 -> x1, Pallas kernels: 206 us -> 201 us  [whole(): pl.pallas_call(functools.partial(whole_kernel, counts), out_shape=jax.Sha...]
where the time goes in v5:
time: 207 us
  Pallas kernels  201 us (97%)
  other arithmetic  3.6 us (2%)
    pallas_call x1, Pallas kernels, whole(): pl.pallas_call(functools.partial(whole_kernel, counts), out_shape=jax.Sha...  201 us

profile of v5, /device:TPU:1, one launch (start us, length us, event | category | flops | bytes accessed | tf_op | source)
XLA Modules:
  0.0 206.7 jit_solution(3036948088327885241)
XLA Ops:
  0.6 0.0 copy-start.1
  0.7 0.1 iota_add_fusion
  0.8 0.1 add.95
  0.8 0.9 reshape.101
  1.7 0.2 fusion
  2.0 0.2 convert_reduce_fusion
  2.2 0.2 select_reduce_fusion
  2.4 0.3 select_reduce_fusion.2
  2.7 0.1 copy.16
  2.8 0.1 reshape.102.refs_2_
  2.9 0.0 copy-start
  2.9 0.7 select_reduce_fusion.1.refs_3_
  3.6 0.7 dynamic-slice_reduce_fusion.refs_1_
  4.3 0.6 select_reduce_fusion.4.refs_0_
  4.8 0.0 copy-done
  4.9 200.5 %whole.1 = f32[2,128]{1,0:T(2,128)} custom-call(s32[16]{0:T(128)} %select_reduce_fusion.4.refs_0_, s32[7]{0:T(128)} %dynamic-slice_reduce_fusion.refs_1_, s32[56]{0:T(128)} %copy-done, s32[56]{0:T(128)} %select_reduce_fusion.1.refs_3_, s32[4]{0:T(128)} %refs_4_.1, bf16[256,5376]{1,0:T(8,128)(2,1)} %refs_5_.1, bf16[7,96,768]{2,1,0:T(8,128)(2,1)} %refs_6_.1, ...), custom_call_target="tpu_custom_call" | custom-call | tf_op jit(solution)/shard_map/whole/pallas_call | solution.py:824
  205.4 0.0 copy-done.1
  205.4 1.3 fusion.8
  (3 shorter events, 0.0 us)
Async XLA Ops:
  0.6 204.8 %copy-start.1 = (f32[16]{0:T(128)S(1)}, f32[16]{0:T(128)}, u32[]{:S(2)}) copy-start(f32[16]{0:T(128)} %param.24) | copy-start | bytes 196
  2.9 2.0 copy-start

commit v6 on v5

--- a/solution.py
+++ b/solution.py
@@ -120,13 +120,31 @@
             sk.at[p, slab, q], vk.at[p, slab, q], sibling(),
         )
 
-    for p in range(3):
-        for step in (1, 3, 2):
+    for step in (1, 3, 2):
+        for p in range(3):
             first(p, step).start()
+
+    def clear(d, carry):
+        acc[d] = jnp.zeros((rows, vocab_rows), jnp.float32)
+        return carry
+
+    lax.fori_loop(0, 128, clear, 0)
+    lanes = lax.broadcasted_iota(jnp.int32, (128, 128), 1)
+    diagonal = lax.broadcasted_iota(jnp.int32, (128, 128), 0) == lanes
+
+    def turn(j, carry):
+        line = jnp.broadcast_to(actions_ref[pl.ds(j, 1)].astype(jnp.float32), (128, 128))
+        turned = jnp.sum(jnp.where(diagonal, line, 0.0), axis=1, keepdims=True)
+        column[pl.ds(j * 8, 8)] = turned.astype(jnp.int32).reshape(8, rows, 1)
+        return carry
+
+    lax.fori_loop(0, actions_ref.shape[0], turn, 0)
+
     for p in range(3):
         for step in (1, 3, 2):
             first(p, step).wait_recv()
-        for step in (3, 1, 2):
+    for step in (3, 1, 2):
+        for p in range(3):
             second(p, step).start()
     for p in range(3):
         for step in (1, 3):
@@ -211,22 +229,27 @@
             tail((near(i // 3), near(i % 3), near(j)))
         return carry
 
-    def late_x(i, carry):
+    def middle_tail(i, carry):
+        for j in range(3):
+            tail((2, near(j), i))
+            tail((i, 2, near(j)))
+            tail((near(j), i, 2))
+        return carry
+
+    def late_tail(i, carry):
         for j in range(4):
-            tail((2, i, j))
-        return carry
-
-    def late_y(i, carry):
-        for j in range(4):
-            tail((near(i), 2, j))
-        return carry
-
-    def late_z(i, carry):
-        for j in range(3):
-            tail((near(i), near(j), 2))
+            tail((2, j, 2 + i))
+        tail((2, 2, i))
+        tail((i, 2, 2))
+        for j in range(2):
+            tail((3, 2, 2 * i + j))
         return carry
 
     def group(g, carry):
+        @pl.when(g == 7)
+        def _():
+            lax.fori_loop(0, 2, middle_tail, 0)
+
         slabs, lines = [slab_of(g, i) for i in range(2)], [row_of(g, i) for i in range(2)]
         for p in range(3):
             for i in range(2):
@@ -263,26 +286,11 @@
                 arrivals(g + 1)
         return carry
 
-    def clear(d, carry):
-        acc[d] = jnp.zeros((rows, vocab_rows), jnp.float32)
-        return carry
-
-    lax.fori_loop(0, 128, clear, 0)
-    lanes = lax.broadcasted_iota(jnp.int32, (128, 128), 1)
-    diagonal = lax.broadcasted_iota(jnp.int32, (128, 128), 0) == lanes
-
-    def turn(j, carry):
-        line = jnp.broadcast_to(actions_ref[pl.ds(j, 1)].astype(jnp.float32), (128, 128))
-        turned = jnp.sum(jnp.where(diagonal, line, 0.0), axis=1, keepdims=True)
-        column[pl.ds(j * 8, 8)] = turned.astype(jnp.int32).reshape(8, rows, 1)
-        return carry
-
-    lax.fori_loop(0, actions_ref.shape[0], turn, 0)
     lax.fori_loop(0, 8, group, 0)
 
-    lax.fori_loop(0, 4, late_x, 0)
-    lax.fori_loop(0, 3, late_y, 0)
-    lax.fori_loop(0, 3, late_z, 0)
+    lax.fori_loop(0, 2, late_tail, 0)
+    for j in range(3):
+        tail((near(j), 3, 2))
     ones = jnp.ones((8, 128), jnp.float32)
     for c in range(8):
         sums = [
@@ -492,18 +500,18 @@
         blocks(body)
 
     def side(i, yy):
-        turn = 4 if yy == 0 else early(i) // 2
+        half = 4 if yy == 0 else early(i) // 2
 
         def body(k):
             z_copy(i, yy, 1, k).wait_recv()
 
-            @pl.when(k < turn)
+            @pl.when(k < half)
             def _():
                 f_copy(i, yy, 1, k).start()
 
             z_copy(i, yy, 3, k).wait_recv()
 
-            @pl.when(k >= turn)
+            @pl.when(k >= half)
             def _():
                 f_copy(i, yy, 3, k).start()
 
@@ -558,10 +566,10 @@
 
     own(0)
     partner(0)
+    side(0, 0)
     own(1)
-    side(0, 0)
+    side(0, 1)
     partner(1)
-    side(0, 1)
     far(0, 0)
     side(1, 0)
     far(0, 1)
@@ -623,12 +631,6 @@
     far(2, 0)
     far(2, 1)
 
-    def order(r, carry):
-        wout[r] = held.at[2].reshape(8 * n_blk, blk_rows, chunk)[slot_of[r]]
-        return carry
-
-    lax.fori_loop(0, depth // blk_rows, order, 0)
-
     share = tokens // 16
     per = wout.shape[0] // half_out.shape[0]
     piece = per * blk_rows
@@ -653,20 +655,30 @@
 
     n_pieces = half_out.shape[0]
 
-    def give(n, carry):
+    def order(r, carry):
+        wout[r] = held.at[2].reshape(8 * n_blk, blk_rows, chunk)[slot_of[r]]
+        return carry
+
+    def give(n):
+        lax.fori_loop(n * per, (n + 1) * per, order, 0)
         half_out[n] = product(1 - core, n).astype(jnp.bfloat16)
         between(n).start()
-        return carry
 
     def take(n, carry):
         mine = product(core, n)
         between(n).wait_recv()
         part_out[n] = (mine + half_in[n].astype(jnp.float32)).astype(jnp.bfloat16)
-        for off in range(1, 8):
+        for off in (2, 6, 1, 4, 3, 7, 5):
             to_chip(n, off).start()
-        return carry
-
-    lax.fori_loop(0, n_pieces, give, 0)
+
+        @pl.when(n + 2 < n_pieces)
+        def _():
+            give(n + 2)
+
+        return carry
+
+    give(0)
+    give(1)
     lax.fori_loop(0, n_pieces, take, 0)
     def swapped(off, carry):
         for i in range(3):

time: 207 us -> 203 us (0.981)
  Pallas kernels: 201 us -> 197 us
    pallas_call x1, Pallas kernels: 201 us -> 197 us  [whole(): pl.pallas_call(functools.partial(whole_kernel, counts), out_shape=jax.Sha...]
where the time goes in v6:
time: 203 us
  Pallas kernels  197 us (97%)
  other arithmetic  3.6 us (2%)
    pallas_call x1, Pallas kernels, whole(): pl.pallas_call(functools.partial(whole_kernel, counts), out_shape=jax.Sha...  197 us

profile of v6, /device:TPU:1, one launch (start us, length us, event | category | flops | bytes accessed | tf_op | source)
XLA Modules:
  0.0 202.9 jit_solution(1183528387757814046)
XLA Ops:
  0.6 0.0 copy-start.1
  0.7 0.1 iota_add_fusion
  0.8 0.1 add.95
  0.8 0.9 reshape.101
  1.7 0.2 fusion
  2.0 0.2 convert_reduce_fusion
  2.2 0.2 select_reduce_fusion
  2.4 0.3 select_reduce_fusion.2
  2.7 0.1 copy.16
  2.8 0.1 reshape.102.refs_2_
  2.9 0.0 copy-start
  2.9 0.7 select_reduce_fusion.1.refs_3_
  3.6 0.7 dynamic-slice_reduce_fusion.refs_1_
  4.3 0.6 select_reduce_fusion.4.refs_0_
  4.8 0.0 copy-done
  4.9 196.7 %whole.1 = f32[2,128]{1,0:T(2,128)} custom-call(s32[16]{0:T(128)} %select_reduce_fusion.4.refs_0_, s32[7]{0:T(128)} %dynamic-slice_reduce_fusion.refs_1_, s32[56]{0:T(128)} %copy-done, s32[56]{0:T(128)} %select_reduce_fusion.1.refs_3_, s32[4]{0:T(128)} %refs_4_.1, bf16[256,5376]{1,0:T(8,128)(2,1)} %refs_5_.1, bf16[7,96,768]{2,1,0:T(8,128)(2,1)} %refs_6_.1, ...), custom_call_target="tpu_custom_call" | custom-call | tf_op jit(solution)/shard_map/whole/pallas_call | solution.py:836
  201.6 0.0 copy-done.1
  201.6 1.3 fusion.8
  (3 shorter events, 0.0 us)
Async XLA Ops:
  0.6 201.0 %copy-start.1 = (f32[16]{0:T(128)S(1)}, f32[16]{0:T(128)}, u32[]{:S(2)}) copy-start(f32[16]{0:T(128)} %param.24) | copy-start | bytes 196
  2.9 2.0 copy-start

commit v7 on v6

--- a/solution.py
+++ b/solution.py
@@ -102,6 +102,13 @@
             s2.at[p, slot], v2.at[p, slot], shifted(axis_of(p, 1), step),
         )
 
+    def second_far(p, step):
+        slot, low = (2, 0) if step == 1 else (1, 2)
+        return send(
+            buf.at[p, 0, slot, core, pl.ds(low, 2)], buf.at[p, 0, 3, core, pl.ds(low, 2)],
+            s2.at[p, step % 3 * 3], v2.at[p, step % 3 * 3], shifted(axis_of(p, 1), step),
+        )
+
     def third(p, q, step):
         return send(
             buf.at[p, 0, q, core], buf.at[p, 4 - step, q, core],
@@ -143,7 +150,7 @@
     for p in range(3):
         for step in (1, 3, 2):
             first(p, step).wait_recv()
-    for step in (3, 1, 2):
+    for step in (3, 1):
         for p in range(3):
             second(p, step).start()
     for p in range(3):
@@ -152,13 +159,19 @@
         across(p, 0, 0).start()
 
     def own_chunk(p, q):
-        second(p, 4 - A2_REL[q]).wait_recv()
+        if q == 3:
+            second_far(p, 1).wait_recv()
+            second_far(p, 3).wait_recv()
+        else:
+            second(p, 4 - A2_REL[q]).wait_recv()
+            second_far(p, 4 - A2_REL[q]).start()
         for step in (1, 3):
             third(p, q, step).start()
         across(p, 0, q).start()
 
-    for p in range(3):
-        own_chunk(p, 1)
+    for q in (1, 2):
+        for p in range(3):
+            own_chunk(p, q)
 
     def slab_of(g, i):
         return jnp.where(g < 2, 0, jnp.where(g > 5, 2, 3 - 2 * i))
@@ -169,9 +182,8 @@
     def arrivals(g):
         @pl.when(g == 1)
         def _():
-            for q in (2, 3):
-                for p in range(3):
-                    own_chunk(p, q)
+            for p in range(3):
+                own_chunk(p, 3)
 
         @pl.when((g > 1) & (g < 6))
         def _():
@@ -327,7 +339,9 @@
     for p in range(3):
         for step in (1, 2, 3):
             first(p, step).wait_send()
+        for step in (1, 3):
             second(p, step).wait_send()
+            second_far(p, step).wait_send()
         for q in range(4):
             third(p, q, 1).wait_send()
             third(p, q, 3).wait_send()
@@ -572,6 +586,7 @@
     partner(1)
     far(0, 0)
     side(1, 0)
+    own(2)
     far(0, 1)
 
     def heads(at, gain):
@@ -600,9 +615,8 @@
             kv[reach - step] = jnp.zeros(kv.shape[1:], kv.dtype)
 
     side(1, 1)
-    own(2)
+    partner(2)
     far(1, 0)
-    partner(2)
     far(1, 1)
     for h in range(2):
         query[h] = heads(h, q_gain)

time: 203 us -> 213 us (1.049)
  Pallas kernels: 197 us -> 207 us
    pallas_call x1, Pallas kernels: 197 us -> 207 us  [whole(): pl.pallas_call(functools.partial(whole_kernel, counts), out_shape=jax.Sha...]
where the time goes in v7:
time: 213 us
  Pallas kernels  207 us (97%)
  other arithmetic  3.6 us (2%)
    pallas_call x1, Pallas kernels, whole(): pl.pallas_call(functools.partial(whole_kernel, counts), out_shape=jax.Sha...  207 us

profile of v7, /device:TPU:1, one launch (start us, length us, event | category | flops | bytes accessed | tf_op | source)
XLA Modules:
  0.0 213.2 jit_solution(395742938445479643)
XLA Ops:
  0.6 0.0 copy-start.1
  0.7 0.1 iota_add_fusion
  0.8 0.1 add.95
  0.8 0.9 reshape.101
  1.7 0.2 fusion
  2.0 0.2 convert_reduce_fusion
  2.2 0.2 select_reduce_fusion
  2.4 0.3 select_reduce_fusion.2
  2.7 0.1 copy.16
  2.8 0.1 reshape.102.refs_2_
  2.9 0.0 copy-start
  2.9 0.7 select_reduce_fusion.1.refs_3_
  3.6 0.7 dynamic-slice_reduce_fusion.refs_1_
  4.3 0.6 select_reduce_fusion.4.refs_0_
  4.8 0.0 copy-done
  4.9 207.1 %whole.1 = f32[2,128]{1,0:T(2,128)} custom-call(s32[16]{0:T(128)} %select_reduce_fusion.4.refs_0_, s32[7]{0:T(128)} %dynamic-slice_reduce_fusion.refs_1_, s32[56]{0:T(128)} %copy-done, s32[56]{0:T(128)} %select_reduce_fusion.1.refs_3_, s32[4]{0:T(128)} %refs_4_.1, bf16[256,5376]{1,0:T(8,128)(2,1)} %refs_5_.1, bf16[7,96,768]{2,1,0:T(8,128)(2,1)} %refs_6_.1, ...), custom_call_target="tpu_custom_call" | custom-call | tf_op jit(solution)/shard_map/whole/pallas_call | solution.py:850
  211.9 0.0 copy-done.1
  212.0 1.3 fusion.8
  (3 shorter events, 0.0 us)
Async XLA Ops:
  0.6 211.3 %copy-start.1 = (f32[16]{0:T(128)S(1)}, f32[16]{0:T(128)}, u32[]{:S(2)}) copy-start(f32[16]{0:T(128)} %param.24) | copy-start | bytes 196
  2.9 2.0 copy-start
